TPU v7x, 32 devices: a whole 2x2x4 slice. The times are simulated.
32 devices in a mesh: groups: 2 (over x), span: 16 (over z, y, core).
Axes of the slice: x: 2, y: 2, z: 4, core: 2. Of those that a mesh axis runs over, the one named last changes fastest.
Arguments:
- queries: bfloat16 [8192, 1024], P(('groups', 'span')), parts along dimension 0, may hold values from -96 to 96
- keys: bfloat16 [8192, 1024], P(('groups', 'span')), parts along dimension 0, may hold values from -9 to 9
- values: bfloat16 [8192, 1024], P(('groups', 'span')), parts along dimension 0, may hold values from -6 to 6
- track: int32 [64, 16], P(('groups', 'span')), parts along dimension 0, may hold values 0 or 1
- out_weight: bfloat16 [1024, 1024], replicated, may hold values from -0.1875 to 0.1875
- grad_out: bfloat16 [8192, 1024], P(('groups', 'span')), parts along dimension 0, may hold values from -6 to 6
Outputs:
- query_grad: bfloat16 [8192, 1024], P(('groups', 'span')), parts along dimension 0
- key_grad: bfloat16 [8192, 1024], P(('groups', 'span')), parts along dimension 0
- value_grad: bfloat16 [8192, 1024], P(('groups', 'span')), parts along dimension 0
- weight_grad: float32 [2048, 1024], P(('groups', 'span')), parts along dimension 0
There are 2 independent parts, one for each index of `groups`. A program takes and returns all parts, laid end to end along the dimension named above; an argument that names none is the same for every part. Nothing has to cross between parts.
All inputs are finite; a program needn't handle non-finite values. No bound on the sum of `track` on one device may be relied on, other than what follows from the above.
Results may differ from a plain program's by a relative error of at most 0.039.
Values may be sent and summed in bfloat16 or wider, within the bound.
No kernel may reach another device: no remote copies, remote signals or barrier semaphores. Data moves between devices by JAX's collectives and lax.ppermute only.
A program may use at most 64 MiB of HBM per device.

v0:
```python
import functools

import jax
import jax.numpy as jnp
from jax import lax
from jax.experimental import pallas as pl
from jax.experimental.pallas import tpu as pltpu
from jax.sharding import PartitionSpec as P

HEADS = 16
BLOCK = 128
WINDOW = 8
ROW = 4
LANES = 128
NEG = -1e30
COUNTS = 24
SPARE, ZERO, SLOTS = 24, 28, 29
VMEM_LIMIT = 16 * 1024 * 1024
SMALL = pl.CostEstimate(flops=1_000_000, bytes_accessed=100_000, transcendentals=0)

F32 = jnp.float32
BF16 = jnp.bfloat16

ANY = pl.BlockSpec(memory_space=pl.ANY)
SMEM = pl.BlockSpec(memory_space=pltpu.SMEM)
VMEM = pl.BlockSpec(memory_space=pltpu.VMEM)


def nn(a, b):
    return lax.dot_general(a, b, (((1,), (0,)), ((), ())), preferred_element_type=F32)


def nt(a, b):
    return lax.dot_general(a, b, (((1,), (1,)), ((), ())), preferred_element_type=F32)


def tn(a, b):
    return lax.dot_general(a, b, (((0,), (0,)), ((), ())), preferred_element_type=F32)


def place():
    index = lax.axis_index("span").astype(jnp.int32)
    return index % ROW, index // ROW


def params():
    return pltpu.CompilerParams(vmem_limit_bytes=VMEM_LIMIT)


def split_pair(a, b):
    lane = lax.broadcasted_iota(jnp.int32, a.shape, 1)
    low = lane < LANES // 2
    even = jnp.where(low, a, pltpu.roll(b, LANES // 2, 1))
    odd = jnp.where(low, pltpu.roll(a, LANES // 2, 1), b)
    return even, odd


def packed(src, chunk, pair):
    r, _ = place()
    odd_me = (r % 2) == 1
    tile = 4 * chunk + (r // 2 + pair) % 2
    a = src[:, pl.ds(pl.multiple_of(tile * LANES, LANES), LANES)].astype(F32)
    b = src[:, pl.ds(pl.multiple_of((tile + 2) * LANES, LANES), LANES)].astype(F32)
    even, odd = split_pair(a, b)
    return jnp.where(odd_me, odd, even), jnp.where(odd_me, even, odd)


def pack_first_kernel(t_v, k_v, v_v, own_ref, o1, o2, o3):
    outs = (o1, o2, o3)
    rows = k_v.shape[0]
    for out in outs:
        out[2 * rows : 2 * rows + 16, :] = jnp.zeros((16, LANES), BF16)
        out[2 * rows : 2 * rows + t_v.shape[0], 0 : t_v.shape[1]] = t_v[...].astype(F32).astype(BF16)
    for which, src in enumerate((k_v, v_v)):
        for side, value in enumerate(packed(src, 1, 0)):
            if side == 0:
                base = (2 + which) * rows
                own_ref[base : base + rows, :] = value.astype(BF16)
        for pair in (0, 1):
            for side, value in enumerate(packed(src, 0, pair)):
                d = 2 * pair + side
                value = value.astype(BF16)
                base = which * rows
                if d == 0:
                    own_ref[base : base + rows, :] = value
                else:
                    outs[d - 1][base : base + rows, :] = value


def pack_second_kernel(q_ref, k_ref, v_ref, *outs):
    rows = k_ref.shape[0]
    for pair in (0, 1):
        for which, src in enumerate((k_ref, v_ref)):
            for side, value in enumerate(packed(src, 1, pair)):
                outs[2 * pair + side][which * rows : (which + 1) * rows, :] = value.astype(BF16)
        for chunk in (0, 1):
            for side, value in enumerate(packed(q_ref, chunk, pair)):
                base = (2 + chunk) * rows
                outs[2 * pair + side][base : base + rows, :] = (value * 0.125).astype(BF16)


def pack_first(track, keys, values):
    rows = keys.shape[0]
    outs = pl.pallas_call(
        pack_first_kernel,
        out_shape=(jax.ShapeDtypeStruct((4 * rows, LANES), BF16),)
        + (jax.ShapeDtypeStruct((2 * rows + 16, LANES), BF16),) * 3,
        in_specs=[VMEM] * 3,
        out_specs=[VMEM] * 4,
        compiler_params=params(),
        cost_estimate=SMALL,
        name="pack_first",
    )(track, keys, values)
    return outs[0], outs[1:]


def pack_second(queries, keys, values):
    rows = queries.shape[0]
    return pl.pallas_call(
        pack_second_kernel,
        out_shape=(jax.ShapeDtypeStruct((4 * rows, LANES), BF16),) * ROW,
        in_specs=[VMEM] * 3,
        out_specs=[VMEM] * ROW,
        compiler_params=params(),
        cost_estimate=SMALL,
        name="pack_second",
    )(queries, keys, values)


def stack_kernel(rows, a, b, c, out):
    for i, src in enumerate((a, b, c)):
        out[i * rows : (i + 1) * rows, :] = src[0:rows, :]


def stack(rows, pieces):
    return pl.pallas_call(
        functools.partial(stack_kernel, rows),
        out_shape=jax.ShapeDtypeStruct((3 * rows, LANES), BF16),
        in_specs=[VMEM] * 3,
        out_specs=VMEM,
        compiler_params=params(),
        cost_estimate=SMALL,
        name="stack",
    )(*pieces)


def grad_kernel(w, g0, g1, g2, g3, out, wide_w):
    r, _ = place()
    half = LANES // 2
    rows = g0.shape[0]
    for j in range(ROW):
        at = pl.multiple_of((ROW * j + r) * half, half)
        wide_w[j * half : (j + 1) * half, :] = w[pl.ds(at, half), :]
    for d, g in enumerate((g0, g1, g2, g3)):
        at = pl.multiple_of((r ^ d) * rows, rows)
        out[pl.ds(at, rows), :] = nt(g[...], wide_w[...]).astype(BF16)


def grad_attn(weight, gos):
    rows, width = gos[0].shape
    return pl.pallas_call(
        grad_kernel,
        out_shape=jax.ShapeDtypeStruct((ROW * rows, 2 * LANES), BF16),
        in_specs=[VMEM] * (1 + ROW),
        out_specs=VMEM,
        scratch_shapes=[pltpu.VMEM((2 * LANES, width), BF16)],
        compiler_params=params(),
        cost_estimate=SMALL,
        name="grad_attn",
    )(weight, *gos)


def plan_kernel(track_ref, list_ref):
    r, z = place()

    def one_query(qi, carry):
        rho = qi // 2
        span = ROW * z + rho
        source = 2 * (r ^ rho) + qi % 2

        near, total = jnp.int32(0), jnp.int32(0)
        for i in range(2 * WINDOW):
            u = span - (i // 2 + 1)
            use = jnp.logical_and(track_ref[source, i] == 1, u >= 0).astype(jnp.int32)
            safe = jnp.maximum(u, 0)
            back = z - safe // ROW
            list_ref[qi, total] = (back * ROW + safe % ROW) * 2 + i % 2
            near = near + jnp.where(back < 2, use, 0)
            total = total + use
        list_ref[qi, COUNTS] = near
        list_ref[qi, COUNTS + 1] = total
        return carry

    lax.fori_loop(0, 2 * ROW, one_query, 0)


def plan(track_row):
    return pl.pallas_call(
        plan_kernel,
        out_shape=jax.ShapeDtypeStruct((2 * ROW, COUNTS + 2), jnp.int32),
        in_specs=[SMEM],
        out_specs=SMEM,
        cost_estimate=SMALL,
        name="plan",
    )(track_row)


def low_lanes(shape):
    return lax.broadcasted_iota(jnp.int32, shape, 1) < LANES // 2


def two_heads(x):
    low, zero = low_lanes(x.shape), jnp.zeros_like(x)
    return jnp.concatenate([jnp.where(low, x, zero), jnp.where(low, zero, x)], axis=0)


def pick(x):
    return jnp.where(low_lanes((BLOCK, LANES)), x[:BLOCK], x[BLOCK:])


def causal(shape):
    query = lax.broadcasted_iota(jnp.int32, shape, 0) % BLOCK
    return lax.broadcasted_iota(jnp.int32, shape, 1) <= query


def gather_row(r, chunk, back, own, rest, kk, vv):
    for d in range(ROW):
        src, base = (own, 512 * chunk) if d == 0 else (rest, 512 * (d - 1))
        for b in (0, 1):
            f = 8 * back + 2 * (r ^ d) + b
            at = base + b * BLOCK
            kk[f] = src[at : at + BLOCK, :]
            vv[f, :, 0:LANES] = src[at + 256 : at + 256 + BLOCK, :]


def gather_queries(r, chunk, seconds, qq):
    for d, second in enumerate(seconds):
        for b in (0, 1):
            at = 512 + chunk * 256 + b * BLOCK
            qq[2 * (r ^ d) + b] = second[at : at + BLOCK, :]


def slots_of(list_ref, qi, start, count, how_many):
    ks, vs = [], []
    for i in range(how_many):
        position = start + i
        inside = position < count
        f = list_ref[qi, jnp.minimum(position, COUNTS - 1)]
        ks.append(jnp.where(inside, f, SPARE + qi // 2))
        vs.append(jnp.where(inside, f, ZERO))
    return ks, vs


def own_slots(rho, b):
    return [2 * rho if b else SPARE + rho, 2 * rho + b], [2 * rho if b else ZERO, 2 * rho + b]


def fwd_group(kk, vv, q2, ks, vs, diag=None):
    scores = nt(q2, jnp.concatenate([kk[f] for f in ks], axis=0))
    parts = [scores[:, i * BLOCK : (i + 1) * BLOCK] for i in range(len(ks))]
    if diag is not None:
        parts[diag] = jnp.where(causal(parts[diag].shape), parts[diag], NEG)
    top = jnp.max(functools.reduce(jnp.maximum, parts), axis=1, keepdims=True)
    expo = jnp.concatenate([jnp.exp(part - top).astype(BF16) for part in parts], axis=1)
    out = nn(expo, jnp.concatenate([vv[f] for f in vs], axis=0))
    return pick(jnp.broadcast_to(top, (2 * BLOCK, LANES))), pick(out[:, LANES:]), pick(out[:, :LANES])


def merge(before, state, qi, group):
    m, l, num = before[0, qi], before[1, qi], before[2, qi]
    top = jnp.maximum(m, group[0])
    old, new = jnp.exp(m - top), jnp.exp(group[0] - top)
    state[0, qi] = top
    state[1, qi] = l * old + group[1] * new
    state[2, qi] = num * old + group[2] * new


NEAR_FIRST = tuple(6 + 2 * (rho // 2) for rho in range(ROW))
FAR_FIRST = tuple(6 - 2 * ((rho + 1) // 2) for rho in range(ROW))
BACK_FIRST = 10


def near_kernel(
    chunk, list_ref, own0, rest0, own1, rest1, s0, s1, s2, s3, after, state, kk, vv, qq
):
    r, _ = place()
    gather_row(r, chunk, 0, own0, rest0, kk, vv)
    gather_row(r, chunk, 1, own1, rest1, kk, vv)
    gather_queries(r, chunk, (s0, s1, s2, s3), qq)
    kk[ZERO] = jnp.zeros((BLOCK, LANES), BF16)
    for f in range(SLOTS):
        if f < SPARE:
            vv[f, :, LANES : 2 * LANES] = jnp.ones((BLOCK, LANES), BF16)
        else:
            vv[f] = jnp.zeros((BLOCK, 2 * LANES), BF16)
    for rho in range(ROW):
        kk[SPARE + rho] = jnp.broadcast_to(kk[2 * rho, 0:1, :], (BLOCK, LANES))
    for qi in range(2 * ROW):
        rho, b = qi // 2, qi % 2
        ks, vs = slots_of(list_ref, qi, 0, list_ref[qi, COUNTS], NEAR_FIRST[rho])
        own_ks, own_vs = own_slots(rho, b)
        group = fwd_group(kk, vv, two_heads(qq[qi]), own_ks + ks, own_vs + vs, diag=1)
        for i, value in enumerate(group):
            state[i, qi] = value

    def overflow(rho, carry):
        first = NEAR_FIRST[0] + 2 * (rho // 2)
        counts = [list_ref[2 * rho + b, COUNTS] for b in (0, 1)]

        def body(g, inner):
            for b in (0, 1):
                qi = 2 * rho + b
                ks, vs = slots_of(list_ref, qi, first + 4 * g, counts[b], 4)
                merge(state, state, qi, fwd_group(kk, vv, two_heads(qq[qi]), ks, vs))
            return inner

        return lax.fori_loop(0, (jnp.maximum(counts[0], counts[1]) - first + 3) // 4, body, carry)

    lax.fori_loop(0, ROW, overflow, 0)


def near(chunk, lists, own0, rest0, own1, rest1, seconds, after):
    return pl.pallas_call(
        functools.partial(near_kernel, chunk),
        out_shape=(
            jax.ShapeDtypeStruct((3, 8, BLOCK, LANES), F32),
            jax.ShapeDtypeStruct((SLOTS, BLOCK, LANES), BF16),
            jax.ShapeDtypeStruct((SLOTS, BLOCK, 2 * LANES), BF16),
            jax.ShapeDtypeStruct((8, BLOCK, LANES), BF16),
        ),
        in_specs=[SMEM] + [VMEM] * 8 + [ANY],
        out_specs=[VMEM] * 4,
        compiler_params=params(),
        cost_estimate=SMALL,
        name=f"near{chunk}",
    )(lists, own0, rest0, own1, rest1, *seconds, after)


def far_kernel(
    chunk, last, list_ref, own2, rest2, g0, g1, g2, g3, after, earlier, state_in, kk_in, vv_in, qq,
    kk, vv, attn_ref, lse_ref, *refs
):
    *terms, state, wide = refs
    r, z = place()
    gather_row(r, chunk, 2, own2, rest2, kk, vv)
    for qi in range(2 * ROW):
        ks, vs = slots_of(
            list_ref, qi, list_ref[qi, COUNTS], list_ref[qi, COUNTS + 1], FAR_FIRST[qi // 2]
        )
        group = fwd_group(kk, vv, two_heads(qq[qi]), ks, vs)
        merge(state_in, state, qi, group)

    def overflow(rho, carry):
        first = FAR_FIRST[0] - 2 * ((rho + 1) // 2)
        starts = [list_ref[2 * rho + b, COUNTS] + first for b in (0, 1)]
        counts = [list_ref[2 * rho + b, COUNTS + 1] for b in (0, 1)]

        def body(g, inner):
            for b in (0, 1):
                qi = 2 * rho + b
                ks, vs = slots_of(list_ref, qi, starts[b] + 4 * g, counts[b], 4)
                merge(state, state, qi, fwd_group(kk, vv, two_heads(qq[qi]), ks, vs))
            return inner

        longest = jnp.maximum(counts[0] - starts[0], counts[1] - starts[1])
        return lax.fori_loop(0, (longest + 3) // 4, body, carry)

    lax.fori_loop(0, ROW, overflow, 0)
    for qi in range(2 * ROW):
        lse_ref[qi] = state[0, qi] + jnp.log(state[1, qi])
        attn_ref[qi * BLOCK : (qi + 1) * BLOCK, :] = (state[2, qi] / state[1, qi]).astype(BF16)
    term = None
    for d, g in enumerate((g0, g1, g2, g3)):
        rows = g.shape[0]
        at = pl.multiple_of((r ^ d) * rows, rows)
        part = tn(attn_ref[pl.ds(at, rows), :], g[...])
        term = part if term is None else term + part
    if not last:
        terms[0][...] = term.astype(BF16)
        return
    wide[0:LANES, :] = earlier[...]
    wide[LANES : 2 * LANES, :] = term.astype(BF16)
    half = LANES // 2
    for delta, out in enumerate(terms):
        at = pl.multiple_of((z + delta) % ROW * half, half)
        out[...] = wide[pl.ds(at, half), :]


def far(chunk, last, lists, own2, rest2, gos, after, earlier, state, kk, vv, qq):
    width = gos[0].shape[1]
    weights = (
        (jax.ShapeDtypeStruct((LANES // 2, width), BF16),) * 4
        if last
        else (jax.ShapeDtypeStruct((LANES, width), BF16),)
    )
    return pl.pallas_call(
        functools.partial(far_kernel, chunk, last),
        out_shape=(
            jax.ShapeDtypeStruct(kk.shape, BF16),
            jax.ShapeDtypeStruct(vv.shape, BF16),
            jax.ShapeDtypeStruct((8 * BLOCK, LANES), BF16),
            jax.ShapeDtypeStruct((8, BLOCK, LANES), F32),
        )
        + weights,
        in_specs=[SMEM] + [VMEM] * 2 + [VMEM] * ROW + [ANY, VMEM if last else ANY] + [VMEM] * 4,
        out_specs=[VMEM] * (4 + len(weights)),
        input_output_aliases={10: 0, 11: 1},
        scratch_shapes=[
            pltpu.VMEM((3, 8, BLOCK, LANES), F32),
            pltpu.VMEM((2 * LANES, width), BF16),
        ],
        compiler_params=params(),
        cost_estimate=SMALL,
        name=f"far{chunk}",
    )(lists, own2, rest2, *gos, after, earlier, state, kk, vv, qq)


def bwd_group(kk, vv, q2, g2, lse, delta, ks, vs, diag=None):
    scores = nt(q2, jnp.concatenate([kk[f] for f in ks], axis=0))
    dprob = nt(g2, jnp.concatenate([vv[f, :, 0:LANES] for f in ks], axis=0))
    probs, dscores = [], []
    for i in range(len(ks)):
        part = scores[:, i * BLOCK : (i + 1) * BLOCK]
        if diag == i:
            part = jnp.where(causal(part.shape), part, NEG)
        prob = jnp.exp(part - lse)
        dscores.append((prob * (dprob[:, i * BLOCK : (i + 1) * BLOCK] - delta)).astype(BF16))
        probs.append(prob)
    out = nn(jnp.concatenate(dscores, axis=1), jnp.concatenate([kk[f] for f in vs], axis=0))
    return probs, dscores, out


def back_kernel(chunk, which_d, list_ref, kk, vv, qq, g_ref, attn_ref, lse_ref, after, *refs):
    *outs, dq = refs
    r, _ = place()

    def query_side(qi):
        at = pl.ds(pl.multiple_of(qi * BLOCK, BLOCK), BLOCK)
        g = g_ref[at, chunk * LANES : (chunk + 1) * LANES]
        product = g.astype(F32) * attn_ref[at, :].astype(F32)
        low = low_lanes(product.shape)
        delta = jnp.concatenate(
            [
                jnp.sum(jnp.where(low, product, 0.0), axis=1, keepdims=True),
                jnp.sum(jnp.where(low, 0.0, product), axis=1, keepdims=True),
            ],
            axis=0,
        )
        half = LANES // 2
        lse = jnp.concatenate([lse_ref[qi, :, 0:1], lse_ref[qi, :, half : half + 1]], axis=0)
        return two_heads(qq[qi]), two_heads(g), lse, delta

    for n, d in enumerate(which_d):
        rho = r ^ d
        sides = [query_side(2 * rho + b) for b in (0, 1)]
        local = []
        for b in (0, 1):
            qi = 2 * rho + b
            ks, vs = slots_of(list_ref, qi, 0, list_ref[qi, COUNTS + 1], BACK_FIRST)
            own_ks, own_vs = own_slots(rho, b)
            probs, dscores, add = bwd_group(kk, vv, *sides[b], own_ks + ks, own_vs + vs, diag=1)
            dq[2 * n + b] = add
            local.append(([p.astype(BF16) for p in probs[:2]], dscores[:2]))
        out = outs[n]
        for which, side in ((1, 0), (0, 1)):
            both = jnp.concatenate([sides[0][side], sides[1][side]], axis=0)
            first = jnp.concatenate([local[0][which][1], local[1][which][0]], axis=0)
            base = 512 if side else 256
            out[base : base + BLOCK, :] = tn(first, both).astype(BF16)
            out[base + BLOCK : base + 256, :] = tn(local[1][which][1], sides[1][side]).astype(BF16)

    def overflow(n, carry):
        rho = r ^ ((n + which_d[0]) % ROW)
        counts = [list_ref[2 * rho + b, COUNTS + 1] for b in (0, 1)]

        def body(g, inner):
            for b in (0, 1):
                qi = 2 * rho + b
                ks, vs = slots_of(list_ref, qi, BACK_FIRST + 4 * g, counts[b], 4)
                _, _, add = bwd_group(kk, vv, *query_side(qi), ks, vs)
                dq[2 * n + b] += add
            return inner

        longest = jnp.maximum(counts[0], counts[1])
        return lax.fori_loop(0, (longest - BACK_FIRST + 3) // 4, body, carry)

    lax.fori_loop(0, len(which_d), overflow, 0)
    for n in range(len(which_d)):
        for b in (0, 1):
            outs[n][b * BLOCK : (b + 1) * BLOCK, :] = (pick(dq[2 * n + b]) * 0.125).astype(BF16)


def back(chunk, which_d, lists, kk, vv, qq, grads, attn, lse, after):
    return pl.pallas_call(
        functools.partial(back_kernel, chunk, which_d),
        out_shape=(jax.ShapeDtypeStruct((768, LANES), BF16),) * len(which_d),
        in_specs=[SMEM] + [VMEM] * 6 + [ANY],
        out_specs=[VMEM] * len(which_d),
        scratch_shapes=[pltpu.VMEM((2 * len(which_d), 2 * BLOCK, LANES), F32)],
        compiler_params=params(),
        cost_estimate=SMALL,
        name=f"back{chunk}_{which_d[0]}",
    )(lists, kk, vv, qq, grads, attn, lse, after)


def unpack_kernel(chunk, *refs):
    ins, outs = refs[:ROW], refs[-3:]
    r, _ = place()
    odd_me = (r % 2) == 1
    rows, width = outs[0].shape
    for pair in (0, 1):
        tile = (r // 2 + pair) % 2
        first, second = ins[2 * pair], ins[2 * pair + 1]
        for which, out in enumerate(outs):
            a = first[which * rows : (which + 1) * rows, :].astype(F32)
            b = second[which * rows : (which + 1) * rows, :].astype(F32)
            low, high = jnp.where(odd_me, b, a), jnp.where(odd_me, a, b)
            one, two = split_pair(low, high)
            out[:, pl.ds(pl.multiple_of(tile * LANES, LANES), LANES)] = one.astype(BF16)
            out[:, pl.ds(pl.multiple_of((tile + 2) * LANES, LANES), LANES)] = two.astype(BF16)


def unpack(chunk, pieces, rows, width, before):
    half = pl.BlockSpec((rows, width // 2), lambda i: (0, chunk))
    return pl.pallas_call(
        functools.partial(unpack_kernel, chunk),
        grid=(1,),
        out_shape=(jax.ShapeDtypeStruct((rows, width), BF16),) * 3,
        in_specs=[VMEM] * ROW + [ANY] * len(before),
        out_specs=[half] * 3,
        input_output_aliases={ROW + i: i for i in range(len(before))},
        compiler_params=params(),
        cost_estimate=SMALL,
        name=f"unpack{chunk}",
    )(*pieces, *before)


def swap(value, axis, bit):
    count = lax.axis_size(axis)
    return lax.ppermute(value, axis, [(s, s ^ bit) for s in range(count)])


def later(value, axis):
    count = lax.axis_size(axis)
    return lax.ppermute(value, axis, [(s, (s + ROW) % count) for s in range(count)])


hold = lax.optimization_barrier


def shards(queries, keys, values, track, out_weight, grad_out):
    rows, width = queries.shape
    count = lax.axis_size("span")
    fast = count == HEADS

    own0, firsts = pack_first(track, keys, values)
    own1 = later(own0, "span")
    got_first = [swap(x, "span", d + 1) for d, x in enumerate(firsts)]
    queries, _ = hold((queries, got_first[0]))
    seconds = list(pack_second(queries, keys, values))
    got_first, _ = hold((got_first, seconds[0]))
    rest0 = [stack(2 * rows, got_first)]
    rest1 = [later(rest0[0], "span")]
    track_row = jnp.concatenate(
        [track.astype(BF16)] + [x[2 * rows : 2 * rows + 2, : 2 * WINDOW] for x in got_first], axis=0
    )
    lists = plan(track_row.astype(jnp.int32))

    seconds, _ = hold((seconds, (rest0[0], own1)))
    seconds[1:] = [swap(seconds[d], "span", d) for d in (1, 2, 3)]
    own2 = later(own1, "span")
    arrived, _ = hold((seconds[1:], (rest1[0], own2, lists)))
    rest0.append(stack(2 * rows, arrived))
    rest1.append(later(rest0[1], "span"))
    grad_late, _ = hold((grad_out, rest0[1]))
    go2 = swap(grad_late, "span", 2)

    stores = [near(0, lists, own0, rest0[0], own1, rest1[0], seconds, lists)]
    first_row, _ = hold((rest1[0], stores[0][0]))
    rest2 = [later(first_row, "span"), later(rest1[1], "span")]
    (grad_late, go2), _ = hold(((grad_out, go2), (stores[0][0], rest1[1])))
    gos = (grad_out, swap(grad_late, "span", 1), go2, swap(go2, "span", 1))
    grads = grad_attn(out_weight, gos)
    stores.append(near(1, lists, own0, rest0[1], own1, rest1[1], seconds, stores[0][0]))

    after = stores[1][0]
    kk, vv, attn, lse, term = far(0, False, lists, own2, rest2[0], gos, after, after, *stores[0])
    out = back(0, (0, 1, 2, 3), lists, kk, vv, stores[0][3], grads, attn, lse, attn)
    pieces = [out[0]] + [swap(out[d], "span", d) for d in (1, 2, 3)]
    grads_out = unpack(0, pieces, rows, width, ())

    kk, vv, attn, lse, *terms = far(1, fast, lists, own2, rest2[1], gos, out[0], term, *stores[1])
    second = (lists, kk, vv, stores[1][3], grads, attn, lse)
    if fast:
        weight_grad = terms[0].astype(F32)
        for delta in (1, 2, 3):
            pairs = [
                (ROW * s + q, ROW * ((s + delta) % ROW) + q) for s in range(ROW) for q in range(ROW)
            ]
            weight_grad += lax.ppermute(terms[delta], "span", pairs).astype(F32)
    else:
        head_dim = width // HEADS
        place_in_row = lax.axis_index("span").astype(jnp.int32) % ROW
        mine = jnp.concatenate([term, terms[0]], axis=0).reshape(ROW, 1, head_dim, width)
        full = jnp.zeros((ROW, ROW, head_dim, width), BF16)
        full = lax.dynamic_update_slice(full, mine, (0, place_in_row, 0, 0)).reshape(width, width)
        weight_grad = lax.psum_scatter(full.astype(F32), "span", scatter_dimension=0, tiled=True)
    out = back(1, (1, 2, 3), *second, attn)
    out, grads_out = hold((out, grads_out))
    crossed = [swap(x, "span", d) for x, d in zip(out, (1, 2, 3))]
    (own,) = back(1, (0,), *second, out[0])
    pieces = [own] + crossed
    query_grad, key_grad, value_grad = unpack(1, pieces, rows, width, grads_out)
    return (query_grad, key_grad, value_grad, weight_grad)


def solution(mesh):
    spec = P(("groups", "span"), None)
    return jax.shard_map(
        shards,
        mesh=mesh,
        in_specs=(spec, spec, spec, spec, P(), spec),
        out_specs=(spec, spec, spec, spec),
        check_vma=False,
    )
```

profile of v0, /device:TPU:11, one launch (start us, length us, event | category | flops | bytes accessed | tf_op | source)
XLA Modules:
  0.0 100.4 jit_solution(17713086556971923866)
XLA Ops:
  0.6 0.0 copy-start.1
  0.6 1.0 %copy-done.1 = bf16[256,1024]{1,0:T(8,128)(2,1)S(1)} copy-done((bf16[256,1024]{1,0:T(8,128)(2,1)S(1)}, bf16[256,1024]{1,0:T(8,128)(2,1)}, u32[]{:S(2)}) %copy-start.1) | copy-done | bytes 524312
  1.7 1.0 %copy-done.3 = bf16[256,1024]{1,0:T(8,128)(2,1)S(1)} copy-done((bf16[256,1024]{1,0:T(8,128)(2,1)S(1)}, bf16[256,1024]{1,0:T(8,128)(2,1)}, u32[]{:S(2)}) %copy-start.3) | copy-done | bytes 524312
  2.7 0.7 copy-done.9
  3.4 0.4 pack_first.1
  3.8 0.0 copy-start
  3.8 0.7 collective-permute-start
  4.6 1.3 %collective-permute-start.1 = (bf16[528,128]{1,0:T(8,128)(2,1)S(1)}, bf16[528,128]{1,0:T(8,128)(2,1)S(1)}, u32[]{:S(2)}, u32[]{:S(2)}) collective-permute-start(bf16[528,128]{1,0:T(8,128)(2,1)S(1)} %get-tuple-element.68), channel_id=1, source_target_pairs={{0,2},{1,3},{2,0},{3,1},{4,6},{5,7},{6,4},{7,5},{8,10},{9,11},{10,... | collective-permute-start | bytes 405512 | tf_op jit(solution)/shard_map/ppermute | solution.py:540
  5.8 0.5 collective-permute-start.2
  6.3 1.3 %collective-permute-start.3 = (bf16[1024,128]{1,0:T(8,128)(2,1)S(1)}, bf16[1024,128]{1,0:T(8,128)(2,1)S(1)}, u32[]{:S(2)}, u32[]{:S(2)}) collective-permute-start(bf16[1024,128]{1,0:T(8,128)(2,1)S(1)} %get-tuple-element.75.own0), channel_id=1, source_target_pairs={{0,4},{1,5},{2,6},{3,7},{4,8},{5,9},{6,10},{7,11},{8,12},{9,13},{1... | collective-permute-start | bytes 786440 | tf_op jit(solution)/shard_map/ppermute | solution.py:545
  7.6 1.0 %copy-done.2 = bf16[256,1024]{1,0:T(8,128)(2,1)S(1)} copy-done((bf16[256,1024]{1,0:T(8,128)(2,1)S(1)}, bf16[256,1024]{1,0:T(8,128)(2,1)}, u32[]{:S(2)}) %copy-start.2) | copy-done | bytes 524312
  8.6 1.0 %copy-done.4 = bf16[256,1024]{1,0:T(8,128)(2,1)S(1)} copy-done((bf16[256,1024]{1,0:T(8,128)(2,1)S(1)}, bf16[256,1024]{1,0:T(8,128)(2,1)}, u32[]{:S(2)}) %copy-start.4) | copy-done | bytes 524312
  9.7 1.0 %copy-done.6 = bf16[256,1024]{1,0:T(8,128)(2,1)S(1)} copy-done((bf16[256,1024]{1,0:T(8,128)(2,1)S(1)}, bf16[256,1024]{1,0:T(8,128)(2,1)}, u32[]{:S(2)}) %copy-start.6) | copy-done | bytes 524312
  10.7 1.3 %pack_second.1 = (bf16[1024,128]{1,0:T(8,128)(2,1)S(1)}, bf16[1024,128]{1,0:T(8,128)(2,1)}, bf16[1024,128]{1,0:T(8,128)(2,1)}, bf16[1024,128]{1,0:T(8,128)(2,1)S(1)}) custom-call(bf16[256,1024]{1,0:T(8,128)(2,1)S(1)} %copy-done.6, bf16[256,1024]{1,0:T(8,128)(2,1)S(1)} %copy-done.2, bf16[256,1024]{1,0:T(8,128)(2,1)S(1)} %copy-done.4), custom_call_target="tpu_custom_call" | custom-call | flops 1000000 | bytes 100000 | tf_op jit(solution)/shard_map/pack_second/pallas_call | solution.py:119
  12.0 1.1 %collective-permute-done.2.c = bf16[528,128]{1,0:T(8,128)(2,1)S(1)} collective-permute-done((bf16[528,128]{1,0:T(8,128)(2,1)S(1)}, bf16[528,128]{1,0:T(8,128)(2,1)S(1)}, u32[]{:S(2)}, u32[]{:S(2)}) %collective-permute-start.2) | collective-permute-done | bytes 135200 | tf_op jit(solution)/shard_map/ppermute | solution.py:540
  13.1 1.3 %collective-permute-start.8 = (bf16[1536,128]{1,0:T(8,128)(2,1)S(1)}, bf16[1536,128]{1,0:T(8,128)(2,1)S(1)}, u32[]{:S(2)}, u32[]{:S(2)}) collective-permute-start(bf16[1536,128]{1,0:T(8,128)(2,1)S(1)} %stack.2.rest0), channel_id=1, source_target_pairs={{0,4},{1,5},{2,6},{3,7},{4,8},{5,9},{6,10},{7,11},{8,12},{9,13},{1... | collective-permute-start | bytes 1179656 | tf_op jit(solution)/shard_map/ppermute | solution.py:545
  14.5 0.0 collective-permute-done.3.own1
  14.5 0.5 collective-permute-start.5
  15.0 1.3 %collective-permute-start.4 = (bf16[1024,128]{1,0:T(8,128)(2,1)S(1)}, bf16[1024,128]{1,0:T(8,128)(2,1)S(1)}, u32[]{:S(2)}, u32[]{:S(2)}) collective-permute-start(bf16[1024,128]{1,0:T(8,128)(2,1)S(1)} %collective-permute-done.3.own1), channel_id=1, source_target_pairs={{0,4},{1,5},{2,6},{3,7},{4,8},{5,9},{6,10},{7,11},{8,12},{9,13},{1... | collective-permute-start | bytes 786440 | tf_op jit(solution)/shard_map/ppermute | solution.py:545
  16.3 1.2 %collective-permute-start.6 = (bf16[1024,128]{1,0:T(8,128)(2,1)}, bf16[1024,128]{1,0:T(8,128)(2,1)S(1)}, u32[]{:S(2)}, u32[]{:S(2)}) collective-permute-start(bf16[1024,128]{1,0:T(8,128)(2,1)} %get-tuple-element.80), channel_id=1, source_target_pairs={{0,2},{1,3},{2,0},{3,1},{4,6},{5,7},{6,4},{7,5},{8,10},{9,11},{10,... | collective-permute-start | bytes 786440 | tf_op jit(solution)/shard_map/ppermute | solution.py:540
  17.5 0.7 collective-permute-start.7
  18.3 0.6 maximum_convert_fusion.track_ref
  18.9 2.3 %plan.1.list_ref.after = s32[8,26]{1,0:T(8,128)} custom-call(s32[8,16]{1,0:T(8,128)} %maximum_convert_fusion.track_ref), custom_call_target="tpu_custom_call" | custom-call | flops 1000000 | bytes 100000 | tf_op jit(solution)/shard_map/plan/pallas_call | solution.py:198
  21.1 8.5 %collective-permute-done.4.own2 = bf16[1024,128]{1,0:T(8,128)(2,1)S(1)} collective-permute-done((bf16[1024,128]{1,0:T(8,128)(2,1)S(1)}, bf16[1024,128]{1,0:T(8,128)(2,1)S(1)}, u32[]{:S(2)}, u32[]{:S(2)}) %collective-permute-start.4) | collective-permute-done | bytes 262176 | tf_op jit(solution)/shard_map/ppermute | solution.py:545
  29.6 0.0 collective-permute-done.5.a.s1
  29.6 0.0 collective-permute-done.6.b.s2
  29.6 0.5 collective-permute-done.7.c.s3
  30.2 0.0 collective-permute-done.8.rest1
  30.2 1.3 %collective-permute-start.11 = (bf16[256,1024]{1,0:T(8,128)(2,1)S(1)}, bf16[256,1024]{1,0:T(8,128)(2,1)S(1)}, u32[]{:S(2)}, u32[]{:S(2)}) collective-permute-start(bf16[256,1024]{1,0:T(8,128)(2,1)S(1)} %copy-done), channel_id=1, source_target_pairs={{0,2},{1,3},{2,0},{3,1},{4,6},{5,7},{6,4},{7,5},{8,10},{9,11},{10,... | collective-permute-start | bytes 1572872 | tf_op jit(solution)/shard_map/ppermute | solution.py:540
  31.5 1.3 %collective-permute-start.9 = (bf16[1536,128]{1,0:T(8,128)(2,1)S(1)}, bf16[1536,128]{1,0:T(8,128)(2,1)S(1)}, u32[]{:S(2)}, u32[]{:S(2)}) collective-permute-start(bf16[1536,128]{1,0:T(8,128)(2,1)S(1)} %stack.3.rest0), channel_id=1, source_target_pairs={{0,4},{1,5},{2,6},{3,7},{4,8},{5,9},{6,10},{7,11},{8,12},{9,13},{1... | collective-permute-start | bytes 1179656 | tf_op jit(solution)/shard_map/ppermute | solution.py:545
  32.8 0.7 copy-done.7
  33.5 5.4 %near0.1 = (f32[3,8,128,128]{3,2,1,0:T(8,128)S(1)}, bf16[29,128,128]{2,1,0:T(8,128)(2,1)S(1)}, bf16[29,128,256]{2,1,0:T(8,128)(2,1)S(1)}, bf16[8,128,128]{2,1,0:T(8,128)(2,1)S(1)}) custom-call(s32[8,26]{1,0:T(8,128)S(1)} %copy-done.7, bf16[1024,128]{1,0:T(8,128)(2,1)S(1)} %get-tuple-element.75.own0, bf16[1536,128]{1,0:T(8,128)(2,1)S(1)} %stack.2.rest0, ...), custom_call_target="tpu_custom_call" | custom-call | flops 1000000 | bytes 100000 | tf_op jit(solution)/shard_map/near0/pallas_call | solution.py:323
  38.9 2.5 %collective-permute-done.9.rest1 = bf16[1536,128]{1,0:T(8,128)(2,1)S(1)} collective-permute-done((bf16[1536,128]{1,0:T(8,128)(2,1)S(1)}, bf16[1536,128]{1,0:T(8,128)(2,1)S(1)}, u32[]{:S(2)}, u32[]{:S(2)}) %collective-permute-start.9) | collective-permute-done | bytes 393248 | tf_op jit(solution)/shard_map/ppermute | solution.py:545
  41.4 2.2 %collective-permute-done.11.g2 = bf16[256,1024]{1,0:T(8,128)(2,1)S(1)} collective-permute-done((bf16[256,1024]{1,0:T(8,128)(2,1)S(1)}, bf16[256,1024]{1,0:T(8,128)(2,1)S(1)}, u32[]{:S(2)}, u32[]{:S(2)}) %collective-permute-start.11) | collective-permute-done | bytes 524320 | tf_op jit(solution)/shard_map/ppermute | solution.py:540
  43.6 1.0 collective-permute-start.12
  44.6 0.0 collective-permute-start.13
  44.6 1.3 %collective-permute-start.14 = (bf16[1536,128]{1,0:T(8,128)(2,1)S(1)}, bf16[1536,128]{1,0:T(8,128)(2,1)S(1)}, u32[]{:S(2)}, u32[]{:S(2)}) collective-permute-start(bf16[1536,128]{1,0:T(8,128)(2,1)S(1)} %collective-permute-done.8.rest1), channel_id=1, source_target_pairs={{0,4},{1,5},{2,6},{3,7},{4,8},{5,9},{6,10},{7,11},{8,12},{9,13},{1... | collective-permute-start | bytes 1179656 | tf_op jit(solution)/shard_map/ppermute | solution.py:545
  45.9 1.8 %collective-permute-start.10 = (bf16[1536,128]{1,0:T(8,128)(2,1)S(1)}, bf16[1536,128]{1,0:T(8,128)(2,1)S(1)}, u32[]{:S(2)}, u32[]{:S(2)}) collective-permute-start(bf16[1536,128]{1,0:T(8,128)(2,1)S(1)} %collective-permute-done.9.rest1), channel_id=1, source_target_pairs={{0,4},{1,5},{2,6},{3,7},{4,8},{5,9},{6,10},{7,11},{8,12},{9,13},{1... | collective-permute-start | bytes 1179656 | tf_op jit(solution)/shard_map/ppermute | solution.py:545
  47.7 5.6 %near1.1 = (f32[3,8,128,128]{3,2,1,0:T(8,128)S(1)}, bf16[29,128,128]{2,1,0:T(8,128)(2,1)S(1)}, bf16[29,128,256]{2,1,0:T(8,128)(2,1)S(1)}, bf16[8,128,128]{2,1,0:T(8,128)(2,1)S(1)}) custom-call(s32[8,26]{1,0:T(8,128)S(1)} %copy-done.7, bf16[1024,128]{1,0:T(8,128)(2,1)S(1)} %get-tuple-element.75.own0, bf16[1536,128]{1,0:T(8,128)(2,1)S(1)} %stack.3.rest0, ...), custom_call_target="tpu_custom_call" | custom-call | flops 1000000 | bytes 100000 | tf_op jit(solution)/shard_map/near1/pallas_call | solution.py:323
  53.3 0.0 copy-start.8
  53.3 0.0 collective-permute-done.12.g1
  53.3 0.0 collective-permute-done.13.g3
  53.4 0.8 grad_attn.1.g_ref
  54.2 1.3 %collective-permute-done.14.rest2 = bf16[1536,128]{1,0:T(8,128)(2,1)S(1)} collective-permute-done((bf16[1536,128]{1,0:T(8,128)(2,1)S(1)}, bf16[1536,128]{1,0:T(8,128)(2,1)S(1)}, u32[]{:S(2)}, u32[]{:S(2)}) %collective-permute-start.14) | collective-permute-done | bytes 393248 | tf_op jit(solution)/shard_map/ppermute | solution.py:545
  55.5 3.4 %far0.1 = (bf16[29,128,128]{2,1,0:T(8,128)(2,1)S(1)}, bf16[29,128,256]{2,1,0:T(8,128)(2,1)S(1)}, bf16[1024,128]{1,0:T(8,128)(2,1)S(1)}, f32[8,128,128]{2,1,0:T(8,128)S(1)}, bf16[128,1024]{1,0:T(8,128)(2,1)S(1)}) custom-call(s32[8,26]{1,0:T(8,128)S(1)} %copy-done.8, ...), custom_call_target="tpu_custom_call", output_to_operand_aliasing={{0}: (10, {}), {1}: (11, {})} | custom-call | flops 1000000 | bytes 100000 | tf_op jit(solution)/shard_map/far0/pallas_call | solution.py:396
  58.8 7.3 %back0_0.1 = (bf16[768,128]{1,0:T(8,128)(2,1)S(1)}, bf16[768,128]{1,0:T(8,128)(2,1)S(1)}, bf16[768,128]{1,0:T(8,128)(2,1)S(1)}, bf16[768,128]{1,0:T(8,128)(2,1)S(1)}) custom-call(s32[8,26]{1,0:T(8,128)S(1)} %copy-done.8, bf16[29,128,128]{2,1,0:T(8,128)(2,1)S(1)} %get-tuple-element.95.kk, bf16[29,128,256]{2,1,0:T(8,128)(2,1)S(1)} %get-tuple-element.96.vv, ...), custom_call_target="tpu_custom_call" | custom-call | flops 1000000 | bytes 100000 | tf_op jit(solution)/shard_map/back0_0/pallas_call | solution.py:494
  66.2 1.7 %collective-permute-start.15 = (bf16[768,128]{1,0:T(8,128)(2,1)S(1)}, bf16[768,128]{1,0:T(8,128)(2,1)S(1)}, u32[]{:S(2)}, u32[]{:S(2)}) collective-permute-start(bf16[768,128]{1,0:T(8,128)(2,1)S(1)} %get-tuple-element.111), channel_id=1, source_target_pairs={{0,1},{1,0},{2,3},{3,2},{4,5},{5,4},{6,7},{7,6},{8,9},{9,8},{10,11... | collective-permute-start | bytes 589832 | tf_op jit(solution)/shard_map/ppermute | solution.py:540
  67.8 1.3 %collective-permute-start.16 = (bf16[768,128]{1,0:T(8,128)(2,1)S(1)}, bf16[768,128]{1,0:T(8,128)(2,1)S(1)}, u32[]{:S(2)}, u32[]{:S(2)}) collective-permute-start(bf16[768,128]{1,0:T(8,128)(2,1)S(1)} %get-tuple-element.112), channel_id=1, source_target_pairs={{0,2},{1,3},{2,0},{3,1},{4,6},{5,7},{6,4},{7,5},{8,10},{9,11},{10,... | collective-permute-start | bytes 589832 | tf_op jit(solution)/shard_map/ppermute | solution.py:540
  69.1 0.4 collective-permute-start.17
  69.5 0.0 collective-permute-done.10.rest2
  69.5 3.4 %far1.1 = (bf16[29,128,128]{2,1,0:T(8,128)(2,1)S(1)}, bf16[29,128,256]{2,1,0:T(8,128)(2,1)S(1)}, bf16[1024,128]{1,0:T(8,128)(2,1)S(1)}, f32[8,128,128]{2,1,0:T(8...) custom-call(s32[8,26]{1,0:T(8,128)S(1)} %copy-done.8, ...), custom_call_target="tpu_custom_call", output_to_operand_aliasing={{0}: (10, {}), {1}: (11, {})} | custom-call | flops 1000000 | bytes 100000 | tf_op jit(solution)/shard_map/far1/pallas_call | solution.py:396
  72.9 3.6 %collective-permute-start.23 = (bf16[64,1024]{1,0:T(8,128)(2,1)S(1)}, bf16[64,1024]{1,0:T(8,128)(2,1)S(1)}, u32[]{:S(2)}, u32[]{:S(2)}) collective-permute-start(bf16[64,1024]{1,0:T(8,128)(2,1)S(1)} %get-tuple-element.129), channel_id=1, source_target_pairs={{0,12},{1,13},{2,14},{3,15},{4,0},{5,1},{6,2},{7,3},{8,4},{9,5},{1... | collective-permute-start | bytes 393224 | tf_op jit(solution)/shard_map/ppermute | solution.py:600
  76.6 1.8 %collective-permute-start.22 = (bf16[64,1024]{1,0:T(8,128)(2,1)S(1)}, bf16[64,1024]{1,0:T(8,128)(2,1)S(1)}, u32[]{:S(2)}, u32[]{:S(2)}) collective-permute-start(bf16[64,1024]{1,0:T(8,128)(2,1)S(1)} %get-tuple-element.128), channel_id=1, source_target_pairs={{0,8},{1,9},{2,10},{3,11},{4,12},{5,13},{6,14},{7,15},{8,0},{9,1},... | collective-permute-start | bytes 393224 | tf_op jit(solution)/shard_map/ppermute | solution.py:600
  78.4 2.3 %collective-permute-start.21 = (bf16[64,1024]{1,0:T(8,128)(2,1)S(1)}, bf16[64,1024]{1,0:T(8,128)(2,1)S(1)}, u32[]{:S(2)}, u32[]{:S(2)}) collective-permute-start(bf16[64,1024]{1,0:T(8,128)(2,1)S(1)} %get-tuple-element.127), channel_id=1, source_target_pairs={{0,4},{1,5},{2,6},{3,7},{4,8},{5,9},{6,10},{7,11},{8,12},{9,13},{1... | collective-permute-start | bytes 393224 | tf_op jit(solution)/shard_map/ppermute | solution.py:600
  80.7 5.5 %back1_1.1 = (bf16[768,128]{1,0:T(8,128)(2,1)S(1)}, bf16[768,128]{1,0:T(8,128)(2,1)S(1)}, bf16[768,128]{1,0:T(8,128)(2,1)S(1)}) custom-call(s32[8,26]{1,0:T(8,128)S(1)} %copy-done.8, bf16[29,128,128]{2,1,0:T(8,128)(2,1)S(1)} %get-tuple-element.104.kk, bf16[29,128,256]{2,1,0:T(8,128)(2,1)S(1)} %get-tuple-element.105.vv, ...), custom_call_target="tpu_custom_call" | custom-call | flops 1000000 | bytes 100000 | tf_op jit(solution)/shard_map/back1_1/pallas_call | solution.py:494
  86.2 1.2 %unpack0.1 = (bf16[256,1024]{1,0:T(8,128)(2,1)}, bf16[256,1024]{1,0:T(8,128)(2,1)}, bf16[256,1024]{1,0:T(8,128)(2,1)}) custom-call(bf16[768,128]{1,0:T(8,128)(2,1)S(1)} %get-tuple-element.99.after.refs_0_, bf16[768,128]{1,0:T(8,128)(2,1)S(1)} %collective-permute-done.15.refs_1_, bf16[768,128]{1,0:T(8,128)(2,1)S(1)} %collective-permute-done.16.refs_2_, ...), custom_call_target="tpu_custom_call" | custom-call | flops 1000000 | bytes 100000 | tf_op jit(solution)/shard_map/unpack0/pallas_call | solution.py:525
  87.4 1.0 collective-permute-start.18
  88.4 1.2 %collective-permute-start.19 = (bf16[768,128]{1,0:T(8,128)(2,1)S(1)}, bf16[768,128]{1,0:T(8,128)(2,1)S(1)}, u32[]{:S(2)}, u32[]{:S(2)}) collective-permute-start(bf16[768,128]{1,0:T(8,128)(2,1)S(1)} %get-tuple-element.118), channel_id=1, source_target_pairs={{0,2},{1,3},{2,0},{3,1},{4,6},{5,7},{6,4},{7,5},{8,10},{9,11},{10,... | collective-permute-start | bytes 589832 | tf_op jit(solution)/shard_map/ppermute | solution.py:540
  89.7 0.4 collective-permute-start.20
  90.1 0.8 convert_add_fusion
  90.8 2.3 %back1_0.1.refs_0_ = bf16[768,128]{1,0:T(8,128)(2,1)S(1)} custom-call(s32[8,26]{1,0:T(8,128)S(1)} %copy-done.8, bf16[29,128,128]{2,1,0:T(8,128)(2,1)S(1)} %get-tuple-element.104.kk, bf16[29,128,256]{2,1,0:T(8,128)(2,1)S(1)} %get-tuple-element.105.vv, bf16[8,128,128]{2,1,0:T(8,128)(2,1)S(1)} %get-tuple-element.103.qq, bf16[1024,256]{1,0:T(8,128)(2,1)S(1)} %grad_attn.1.g_ref, ...), custom_call_target="tpu_custom_call" | custom-call | flops 1000000 | bytes 100000 | tf_op jit(solution)/shard_map/back1_0/pallas_call | solution.py:494
  93.2 1.8 %collective-permute-done.19.refs_2_ = bf16[768,128]{1,0:T(8,128)(2,1)S(1)} collective-permute-done((bf16[768,128]{1,0:T(8,128)(2,1)S(1)}, bf16[768,128]{1,0:T(8,128)(2,1)S(1)}, u32[]{:S(2)}, u32[]{:S(2)}) %collective-permute-start.19) | collective-permute-done | bytes 196640 | tf_op jit(solution)/shard_map/ppermute | solution.py:540
  94.9 4.3 %collective-permute-done.20.refs_3_ = bf16[768,128]{1,0:T(8,128)(2,1)S(1)} collective-permute-done((bf16[768,128]{1,0:T(8,128)(2,1)S(1)}, bf16[768,128]{1,0:T(8,128)(2,1)S(1)}, u32[]{:S(2)}, u32[]{:S(2)}) %collective-permute-start.20) | collective-permute-done | bytes 196640 | tf_op jit(solution)/shard_map/ppermute | solution.py:540
  99.2 1.2 %unpack1.1 = (bf16[256,1024]{1,0:T(8,128)(2,1)}, bf16[256,1024]{1,0:T(8,128)(2,1)}, bf16[256,1024]{1,0:T(8,128)(2,1)}) custom-call(bf16[768,128]{1,0:T(8,128)(2,1)S(1)} %back1_0.1.refs_0_, bf16[768,128]{1,0:T(8,128)(2,1)S(1)} %collective-permute-done.18.refs_1_, ...), custom_call_target="tpu_custom_call", output_to_operand_aliasing={{0}: (4, {}), {1}: (5, {}), {2}: (6, {})} | custom-call | flops 1000000 | bytes 100000 | tf_op jit(solution)/shard_map/unpack1/pallas_call | solution.py:525
  (27 shorter events, 0.1 us)
Async XLA Ops:
  0.6 1.0 %copy-start.1 = (bf16[256,1024]{1,0:T(8,128)(2,1)S(1)}, bf16[256,1024]{1,0:T(8,128)(2,1)}, u32[]{:S(2)}) copy-start(bf16[256,1024]{1,0:T(8,128)(2,1)} %k_ref.1) | copy-start | bytes 1572868
  1.7 1.0 %copy-start.3 = (bf16[256,1024]{1,0:T(8,128)(2,1)S(1)}, bf16[256,1024]{1,0:T(8,128)(2,1)}, u32[]{:S(2)}) copy-start(bf16[256,1024]{1,0:T(8,128)(2,1)} %v_ref.1) | copy-start | bytes 1572868
  2.7 0.7 copy-start.9
  3.4 14.8 %copy-start.10 = (s32[2,16]{1,0:T(2,128)S(1)}, s32[2,16]{1,0:T(2,128)}, u32[]{:S(2)}) copy-start(s32[2,16]{1,0:T(2,128)} %t_v.1) | copy-start | bytes 388
  3.8 26.4 %copy-start = (bf16[256,1024]{1,0:T(8,128)(2,1)S(1)}, bf16[256,1024]{1,0:T(8,128)(2,1)}, u32[]{:S(2)}) copy-start(bf16[256,1024]{1,0:T(8,128)(2,1)} %g0.5) | copy-start | bytes 1572868
  3.8 3.8 %collective-permute-start = (bf16[528,128]{1,0:T(8,128)(2,1)S(1)}, bf16[528,128]{1,0:T(8,128)(2,1)S(1)}, u32[]{:S(2)}, u32[]{:S(2)}) collective-permute-start(bf16[528,128]{1,0:T(8,128)(2,1)S(1)} %get-tuple-element.67), channel_id=1, source_target_pairs={{0,1},{1,0},{2,3},{3,2},{4,5},{5,4},{6,7},{7,6},{8,9},{9,8},{10,11... | collective-permute-start | bytes 405512 | tf_op jit(solution)/shard_map/ppermute | solution.py:540
  4.6 7.4 %collective-permute-start.1 = (bf16[528,128]{1,0:T(8,128)(2,1)S(1)}, bf16[528,128]{1,0:T(8,128)(2,1)S(1)}, u32[]{:S(2)}, u32[]{:S(2)}) collective-permute-start(bf16[528,128]{1,0:T(8,128)(2,1)S(1)} %get-tuple-element.68), channel_id=1, source_target_pairs={{0,2},{1,3},{2,0},{3,1},{4,6},{5,7},{6,4},{7,5},{8,10},{9,11},{10,... | collective-permute-start | bytes 405512 | tf_op jit(solution)/shard_map/ppermute | solution.py:540
  5.8 7.3 %collective-permute-start.2 = (bf16[528,128]{1,0:T(8,128)(2,1)S(1)}, bf16[528,128]{1,0:T(8,128)(2,1)S(1)}, u32[]{:S(2)}, u32[]{:S(2)}) collective-permute-start(bf16[528,128]{1,0:T(8,128)(2,1)S(1)} %get-tuple-element.69), channel_id=1, source_target_pairs={{0,3},{1,2},{2,1},{3,0},{4,7},{5,6},{6,5},{7,4},{8,11},{9,10},{10,... | collective-permute-start | bytes 405512 | tf_op jit(solution)/shard_map/ppermute | solution.py:540
  6.3 8.2 %collective-permute-start.3 = (bf16[1024,128]{1,0:T(8,128)(2,1)S(1)}, bf16[1024,128]{1,0:T(8,128)(2,1)S(1)}, u32[]{:S(2)}, u32[]{:S(2)}) collective-permute-start(bf16[1024,128]{1,0:T(8,128)(2,1)S(1)} %get-tuple-element.75.own0), channel_id=1, source_target_pairs={{0,4},{1,5},{2,6},{3,7},{4,8},{5,9},{6,10},{7,11},{8,12},{9,13},{1... | collective-permute-start | bytes 786440 | tf_op jit(solution)/shard_map/ppermute | solution.py:545
  7.6 1.0 %copy-start.2 = (bf16[256,1024]{1,0:T(8,128)(2,1)S(1)}, bf16[256,1024]{1,0:T(8,128)(2,1)}, u32[]{:S(2)}) copy-start(bf16[256,1024]{1,0:T(8,128)(2,1)} %k_ref.1) | copy-start | bytes 1572868
  8.6 1.0 %copy-start.4 = (bf16[256,1024]{1,0:T(8,128)(2,1)S(1)}, bf16[256,1024]{1,0:T(8,128)(2,1)}, u32[]{:S(2)}) copy-start(bf16[256,1024]{1,0:T(8,128)(2,1)} %v_ref.1) | copy-start | bytes 1572868
  9.7 1.0 %copy-start.6 = (bf16[256,1024]{1,0:T(8,128)(2,1)S(1)}, bf16[256,1024]{1,0:T(8,128)(2,1)}, u32[]{:S(2)}) copy-start(bf16[256,1024]{1,0:T(8,128)(2,1)} %q_ref) | copy-start | bytes 1572868
  13.1 17.0 %collective-permute-start.8 = (bf16[1536,128]{1,0:T(8,128)(2,1)S(1)}, bf16[1536,128]{1,0:T(8,128)(2,1)S(1)}, u32[]{:S(2)}, u32[]{:S(2)}) collective-permute-start(bf16[1536,128]{1,0:T(8,128)(2,1)S(1)} %stack.2.rest0), channel_id=1, source_target_pairs={{0,4},{1,5},{2,6},{3,7},{4,8},{5,9},{6,10},{7,11},{8,12},{9,13},{1... | collective-permute-start | bytes 1179656 | tf_op jit(solution)/shard_map/ppermute | solution.py:545
  14.5 15.1 %collective-permute-start.5 = (bf16[1024,128]{1,0:T(8,128)(2,1)}, bf16[1024,128]{1,0:T(8,128)(2,1)S(1)}, u32[]{:S(2)}, u32[]{:S(2)}) collective-permute-start(bf16[1024,128]{1,0:T(8,128)(2,1)} %get-tuple-element.79), channel_id=1, source_target_pairs={{0,1},{1,0},{2,3},{3,2},{4,5},{5,4},{6,7},{7,6},{8,9},{9,8},{10,11... | collective-permute-start | bytes 786440 | tf_op jit(solution)/shard_map/ppermute | solution.py:540
  15.0 14.6 %collective-permute-start.4 = (bf16[1024,128]{1,0:T(8,128)(2,1)S(1)}, bf16[1024,128]{1,0:T(8,128)(2,1)S(1)}, u32[]{:S(2)}, u32[]{:S(2)}) collective-permute-start(bf16[1024,128]{1,0:T(8,128)(2,1)S(1)} %collective-permute-done.3.own1), channel_id=1, source_target_pairs={{0,4},{1,5},{2,6},{3,7},{4,8},{5,9},{6,10},{7,11},{8,12},{9,13},{1... | collective-permute-start | bytes 786440 | tf_op jit(solution)/shard_map/ppermute | solution.py:545
  16.3 13.3 %collective-permute-start.6 = (bf16[1024,128]{1,0:T(8,128)(2,1)}, bf16[1024,128]{1,0:T(8,128)(2,1)S(1)}, u32[]{:S(2)}, u32[]{:S(2)}) collective-permute-start(bf16[1024,128]{1,0:T(8,128)(2,1)} %get-tuple-element.80), channel_id=1, source_target_pairs={{0,2},{1,3},{2,0},{3,1},{4,6},{5,7},{6,4},{7,5},{8,10},{9,11},{10,... | collective-permute-start | bytes 786440 | tf_op jit(solution)/shard_map/ppermute | solution.py:540
  17.5 12.6 %collective-permute-start.7 = (bf16[1024,128]{1,0:T(8,128)(2,1)S(1)}, bf16[1024,128]{1,0:T(8,128)(2,1)S(1)}, u32[]{:S(2)}, u32[]{:S(2)}) collective-permute-start(bf16[1024,128]{1,0:T(8,128)(2,1)S(1)} %get-tuple-element.81), channel_id=1, source_target_pairs={{0,3},{1,2},{2,1},{3,0},{4,7},{5,6},{6,5},{7,4},{8,11},{9,10},{10,... | collective-permute-start | bytes 786440 | tf_op jit(solution)/shard_map/ppermute | solution.py:540
  30.2 13.4 %collective-permute-start.11 = (bf16[256,1024]{1,0:T(8,128)(2,1)S(1)}, bf16[256,1024]{1,0:T(8,128)(2,1)S(1)}, u32[]{:S(2)}, u32[]{:S(2)}) collective-permute-start(bf16[256,1024]{1,0:T(8,128)(2,1)S(1)} %copy-done), channel_id=1, source_target_pairs={{0,2},{1,3},{2,0},{3,1},{4,6},{5,7},{6,4},{7,5},{8,10},{9,11},{10,... | collective-permute-start | bytes 1572872 | tf_op jit(solution)/shard_map/ppermute | solution.py:540
  31.5 9.9 %collective-permute-start.9 = (bf16[1536,128]{1,0:T(8,128)(2,1)S(1)}, bf16[1536,128]{1,0:T(8,128)(2,1)S(1)}, u32[]{:S(2)}, u32[]{:S(2)}) collective-permute-start(bf16[1536,128]{1,0:T(8,128)(2,1)S(1)} %stack.3.rest0), channel_id=1, source_target_pairs={{0,4},{1,5},{2,6},{3,7},{4,8},{5,9},{6,10},{7,11},{8,12},{9,13},{1... | collective-permute-start | bytes 1179656 | tf_op jit(solution)/shard_map/ppermute | solution.py:545
  32.8 0.7 copy-start.7
  43.6 9.7 %copy-start.5 = (bf16[1024,1024]{1,0:T(8,128)(2,1)S(1)}, bf16[1024,1024]{1,0:T(8,128)(2,1)}, u32[]{:S(2)}) copy-start(bf16[1024,1024]{1,0:T(8,128)(2,1)} %w.1) | copy-start | bytes 6291460
  43.6 9.7 %collective-permute-start.12 = (bf16[256,1024]{1,0:T(8,128)(2,1)S(1)}, bf16[256,1024]{1,0:T(8,128)(2,1)S(1)}, u32[]{:S(2)}, u32[]{:S(2)}) collective-permute-start(bf16[256,1024]{1,0:T(8,128)(2,1)S(1)} %copy-done), channel_id=1, source_target_pairs={{0,1},{1,0},{2,3},{3,2},{4,5},{5,4},{6,7},{7,6},{8,9},{9,8},{10,11... | collective-permute-start | bytes 1572872 | tf_op jit(solution)/shard_map/ppermute | solution.py:540
  44.6 8.7 %collective-permute-start.13 = (bf16[256,1024]{1,0:T(8,128)(2,1)S(1)}, bf16[256,1024]{1,0:T(8,128)(2,1)S(1)}, u32[]{:S(2)}, u32[]{:S(2)}) collective-permute-start(bf16[256,1024]{1,0:T(8,128)(2,1)S(1)} %collective-permute-done.11.g2), channel_id=1, source_target_pairs={{0,1},{1,0},{2,3},{3,2},{4,5},{5,4},{6,7},{7,6},{8,9},{9,8},{10,11... | collective-permute-start | bytes 1572872 | tf_op jit(solution)/shard_map/ppermute | solution.py:540
  44.6 10.8 %collective-permute-start.14 = (bf16[1536,128]{1,0:T(8,128)(2,1)S(1)}, bf16[1536,128]{1,0:T(8,128)(2,1)S(1)}, u32[]{:S(2)}, u32[]{:S(2)}) collective-permute-start(bf16[1536,128]{1,0:T(8,128)(2,1)S(1)} %collective-permute-done.8.rest1), channel_id=1, source_target_pairs={{0,4},{1,5},{2,6},{3,7},{4,8},{5,9},{6,10},{7,11},{8,12},{9,13},{1... | collective-permute-start | bytes 1179656 | tf_op jit(solution)/shard_map/ppermute | solution.py:545
  45.9 23.6 %collective-permute-start.10 = (bf16[1536,128]{1,0:T(8,128)(2,1)S(1)}, bf16[1536,128]{1,0:T(8,128)(2,1)S(1)}, u32[]{:S(2)}, u32[]{:S(2)}) collective-permute-start(bf16[1536,128]{1,0:T(8,128)(2,1)S(1)} %collective-permute-done.9.rest1), channel_id=1, source_target_pairs={{0,4},{1,5},{2,6},{3,7},{4,8},{5,9},{6,10},{7,11},{8,12},{9,13},{1... | collective-permute-start | bytes 1179656 | tf_op jit(solution)/shard_map/ppermute | solution.py:545
  53.3 2.1 %copy-start.8 = (s32[8,26]{1,0:T(8,128)S(1)}, s32[8,26]{1,0:T(8,128)}, u32[]{:S(2)}) copy-start(s32[8,26]{1,0:T(8,128)} %plan.1.list_ref.after) | copy-start | bytes 2500
  66.2 12.2 %collective-permute-start.15 = (bf16[768,128]{1,0:T(8,128)(2,1)S(1)}, bf16[768,128]{1,0:T(8,128)(2,1)S(1)}, u32[]{:S(2)}, u32[]{:S(2)}) collective-permute-start(bf16[768,128]{1,0:T(8,128)(2,1)S(1)} %get-tuple-element.111), channel_id=1, source_target_pairs={{0,1},{1,0},{2,3},{3,2},{4,5},{5,4},{6,7},{7,6},{8,9},{9,8},{10,11... | collective-permute-start | bytes 589832 | tf_op jit(solution)/shard_map/ppermute | solution.py:540
  67.8 18.4 %collective-permute-start.16 = (bf16[768,128]{1,0:T(8,128)(2,1)S(1)}, bf16[768,128]{1,0:T(8,128)(2,1)S(1)}, u32[]{:S(2)}, u32[]{:S(2)}) collective-permute-start(bf16[768,128]{1,0:T(8,128)(2,1)S(1)} %get-tuple-element.112), channel_id=1, source_target_pairs={{0,2},{1,3},{2,0},{3,1},{4,6},{5,7},{6,4},{7,5},{8,10},{9,11},{10,... | collective-permute-start | bytes 589832 | tf_op jit(solution)/shard_map/ppermute | solution.py:540
  69.1 17.1 %collective-permute-start.17 = (bf16[768,128]{1,0:T(8,128)(2,1)S(1)}, bf16[768,128]{1,0:T(8,128)(2,1)S(1)}, u32[]{:S(2)}, u32[]{:S(2)}) collective-permute-start(bf16[768,128]{1,0:T(8,128)(2,1)S(1)} %get-tuple-element.113), channel_id=1, source_target_pairs={{0,3},{1,2},{2,1},{3,0},{4,7},{5,6},{6,5},{7,4},{8,11},{9,10},{10,... | collective-permute-start | bytes 589832 | tf_op jit(solution)/shard_map/ppermute | solution.py:540
  72.9 16.7 %collective-permute-start.23 = (bf16[64,1024]{1,0:T(8,128)(2,1)S(1)}, bf16[64,1024]{1,0:T(8,128)(2,1)S(1)}, u32[]{:S(2)}, u32[]{:S(2)}) collective-permute-start(bf16[64,1024]{1,0:T(8,128)(2,1)S(1)} %get-tuple-element.129), channel_id=1, source_target_pairs={{0,12},{1,13},{2,14},{3,15},{4,0},{5,1},{6,2},{7,3},{8,4},{9,5},{1... | collective-permute-start | bytes 393224 | tf_op jit(solution)/shard_map/ppermute | solution.py:600
  76.6 13.5 %collective-permute-start.22 = (bf16[64,1024]{1,0:T(8,128)(2,1)S(1)}, bf16[64,1024]{1,0:T(8,128)(2,1)S(1)}, u32[]{:S(2)}, u32[]{:S(2)}) collective-permute-start(bf16[64,1024]{1,0:T(8,128)(2,1)S(1)} %get-tuple-element.128), channel_id=1, source_target_pairs={{0,8},{1,9},{2,10},{3,11},{4,12},{5,13},{6,14},{7,15},{8,0},{9,1},... | collective-permute-start | bytes 393224 | tf_op jit(solution)/shard_map/ppermute | solution.py:600
  78.4 11.7 %collective-permute-start.21 = (bf16[64,1024]{1,0:T(8,128)(2,1)S(1)}, bf16[64,1024]{1,0:T(8,128)(2,1)S(1)}, u32[]{:S(2)}, u32[]{:S(2)}) collective-permute-start(bf16[64,1024]{1,0:T(8,128)(2,1)S(1)} %get-tuple-element.127), channel_id=1, source_target_pairs={{0,4},{1,5},{2,6},{3,7},{4,8},{5,9},{6,10},{7,11},{8,12},{9,13},{1... | collective-permute-start | bytes 393224 | tf_op jit(solution)/shard_map/ppermute | solution.py:600
  87.4 5.7 %collective-permute-start.18 = (bf16[768,128]{1,0:T(8,128)(2,1)S(1)}, bf16[768,128]{1,0:T(8,128)(2,1)S(1)}, u32[]{:S(2)}, u32[]{:S(2)}) collective-permute-start(bf16[768,128]{1,0:T(8,128)(2,1)S(1)} %get-tuple-element.117.after), channel_id=1, source_target_pairs={{0,1},{1,0},{2,3},{3,2},{4,5},{5,4},{6,7},{7,6},{8,9},{9,8},{10,11... | collective-permute-start | bytes 589832 | tf_op jit(solution)/shard_map/ppermute | solution.py:540
  88.4 6.5 %collective-permute-start.19 = (bf16[768,128]{1,0:T(8,128)(2,1)S(1)}, bf16[768,128]{1,0:T(8,128)(2,1)S(1)}, u32[]{:S(2)}, u32[]{:S(2)}) collective-permute-start(bf16[768,128]{1,0:T(8,128)(2,1)S(1)} %get-tuple-element.118), channel_id=1, source_target_pairs={{0,2},{1,3},{2,0},{3,1},{4,6},{5,7},{6,4},{7,5},{8,10},{9,11},{10,... | collective-permute-start | bytes 589832 | tf_op jit(solution)/shard_map/ppermute | solution.py:540
  89.7 9.6 %collective-permute-start.20 = (bf16[768,128]{1,0:T(8,128)(2,1)S(1)}, bf16[768,128]{1,0:T(8,128)(2,1)S(1)}, u32[]{:S(2)}, u32[]{:S(2)}) collective-permute-start(bf16[768,128]{1,0:T(8,128)(2,1)S(1)} %get-tuple-element.119), channel_id=1, source_target_pairs={{0,3},{1,2},{2,1},{3,0},{4,7},{5,6},{6,5},{7,4},{8,11},{9,10},{10,... | collective-permute-start | bytes 589832 | tf_op jit(solution)/shard_map/ppermute | solution.py:540
where the time goes:
time: 101 us; the launch traced here: 100 us
  Pallas kernels  40.1 us (40%)
  starting transfers between devices  29.3 us (29%)
  waiting for transfers between devices  22.3 us (22%)
  local copies, waits for them, and re-layouts  6.59 us (7%)
  other arithmetic  1.38 us (1%)
    pallas_call x3, Pallas kernels, back(): pl.pallas_call(functools.partial(back_kernel, chunk, which_d), out_shape=...  15.1 us
    ppermute x15, starting transfers between devices, swap(): return lax.ppermute(value, axis, [(s, s ^ bit) for s in range(count)])  13.2 us
    ppermute x6, waiting for transfers between devices, later(): lax.ppermute(value, axis, [(s, (s + ROW) % count) for s in range(count)])  12.3 us
    pallas_call x2, Pallas kernels, near(): pl.pallas_call(functools.partial(near_kernel, chunk), out_shape=(jax.Shap...  11 us
    ppermute x15, waiting for transfers between devices, swap(): return lax.ppermute(value, axis, [(s, s ^ bit) for s in range(count)])  9.93 us
    ppermute x6, starting transfers between devices, later(): lax.ppermute(value, axis, [(s, (s + ROW) % count) for s in range(count)])  8.33 us
    ppermute x3, starting transfers between devices, shards(): weight_grad += lax.ppermute(terms[delta], 'span', pairs).astype(F32)  7.74 us
    pallas_call x2, Pallas kernels, far(): pl.pallas_call(functools.partial(far_kernel, chunk, last), out_shape=(jax...  6.77 us
  transfers between devices with their start and end apart: 24, of which 8 were waited for; matrix products, arithmetic and copies ran while one was open for 1% of the time, Pallas kernels for 38%

commit v1 on v0

--- a/solution.py
+++ b/solution.py
@@ -47,6 +47,10 @@
     return pltpu.CompilerParams(vmem_limit_bytes=VMEM_LIMIT)
 
 
+def micros(time):
+    return pl.CostEstimate(flops=int(time * 1.1e9), bytes_accessed=100_000, transcendentals=0)
+
+
 def split_pair(a, b):
     lane = lax.broadcasted_iota(jnp.int32, a.shape, 1)
     low = lane < LANES // 2
@@ -65,12 +69,9 @@
     return jnp.where(odd_me, odd, even), jnp.where(odd_me, even, odd)
 
 
-def pack_first_kernel(t_v, k_v, v_v, own_ref, o1, o2, o3):
+def pack_first_kernel(k_v, v_v, own_ref, o1, o2, o3):
     outs = (o1, o2, o3)
     rows = k_v.shape[0]
-    for out in outs:
-        out[2 * rows : 2 * rows + 16, :] = jnp.zeros((16, LANES), BF16)
-        out[2 * rows : 2 * rows + t_v.shape[0], 0 : t_v.shape[1]] = t_v[...].astype(F32).astype(BF16)
     for which, src in enumerate((k_v, v_v)):
         for side, value in enumerate(packed(src, 1, 0)):
             if side == 0:
@@ -87,44 +88,50 @@
                     outs[d - 1][base : base + rows, :] = value
 
 
-def pack_second_kernel(q_ref, k_ref, v_ref, *outs):
+def pack_second_kernel(t_ref, q_ref, k_ref, v_ref, k1, k2, k3, *q_outs):
     rows = k_ref.shape[0]
+    for out in (k1, k2, k3):
+        out[2 * rows : 2 * rows + 16, :] = jnp.zeros((16, LANES), BF16)
+        out[2 * rows : 2 * rows + t_ref.shape[0], 0 : t_ref.shape[1]] = t_ref[...].astype(F32).astype(BF16)
     for pair in (0, 1):
         for which, src in enumerate((k_ref, v_ref)):
             for side, value in enumerate(packed(src, 1, pair)):
-                outs[2 * pair + side][which * rows : (which + 1) * rows, :] = value.astype(BF16)
+                d = 2 * pair + side
+                if d > 0:
+                    (k1, k2, k3)[d - 1][which * rows : (which + 1) * rows, :] = value.astype(BF16)
         for chunk in (0, 1):
             for side, value in enumerate(packed(q_ref, chunk, pair)):
-                base = (2 + chunk) * rows
-                outs[2 * pair + side][base : base + rows, :] = (value * 0.125).astype(BF16)
-
-
-def pack_first(track, keys, values):
+                q_outs[2 * pair + side][chunk * rows : (chunk + 1) * rows, :] = (value * 0.125).astype(BF16)
+
+
+def pack_first(keys, values):
     rows = keys.shape[0]
     outs = pl.pallas_call(
         pack_first_kernel,
         out_shape=(jax.ShapeDtypeStruct((4 * rows, LANES), BF16),)
-        + (jax.ShapeDtypeStruct((2 * rows + 16, LANES), BF16),) * 3,
-        in_specs=[VMEM] * 3,
+        + (jax.ShapeDtypeStruct((2 * rows, LANES), BF16),) * 3,
+        in_specs=[VMEM] * 2,
         out_specs=[VMEM] * 4,
         compiler_params=params(),
         cost_estimate=SMALL,
         name="pack_first",
-    )(track, keys, values)
+    )(keys, values)
     return outs[0], outs[1:]
 
 
-def pack_second(queries, keys, values):
+def pack_second(track, queries, keys, values):
     rows = queries.shape[0]
-    return pl.pallas_call(
+    outs = pl.pallas_call(
         pack_second_kernel,
-        out_shape=(jax.ShapeDtypeStruct((4 * rows, LANES), BF16),) * ROW,
-        in_specs=[VMEM] * 3,
-        out_specs=[VMEM] * ROW,
+        out_shape=(jax.ShapeDtypeStruct((2 * rows + 16, LANES), BF16),) * 3
+        + (jax.ShapeDtypeStruct((2 * rows, LANES), BF16),) * ROW,
+        in_specs=[VMEM] * 4,
+        out_specs=[VMEM] * (2 * ROW - 1),
         compiler_params=params(),
         cost_estimate=SMALL,
         name="pack_second",
-    )(queries, keys, values)
+    )(track, queries, keys, values)
+    return outs[:3], list(outs[3:])
 
 
 def stack_kernel(rows, a, b, c, out):
@@ -236,7 +243,7 @@
 def gather_queries(r, chunk, seconds, qq):
     for d, second in enumerate(seconds):
         for b in (0, 1):
-            at = 512 + chunk * 256 + b * BLOCK
+            at = chunk * 256 + b * BLOCK
             qq[2 * (r ^ d) + b] = second[at : at + BLOCK, :]
 
 
@@ -331,16 +338,18 @@
         in_specs=[SMEM] + [VMEM] * 8 + [ANY],
         out_specs=[VMEM] * 4,
         compiler_params=params(),
-        cost_estimate=SMALL,
+        cost_estimate=SMALL if chunk else micros(5.5),
         name=f"near{chunk}",
     )(lists, own0, rest0, own1, rest1, *seconds, after)
 
 
 def far_kernel(
-    chunk, last, list_ref, own2, rest2, g0, g1, g2, g3, after, earlier, state_in, kk_in, vv_in, qq,
-    kk, vv, attn_ref, lse_ref, *refs
+    chunk, last, list_ref, own2, rest2, after, state_in, kk_in, vv_in, qq, *refs
 ):
-    *terms, state, wide = refs
+    if last:
+        earlier, *gos = refs[: 1 + ROW]
+        refs = refs[1 + ROW :]
+    kk, vv, attn_ref, lse_ref, *terms, state, wide = refs
     r, z = place()
     gather_row(r, chunk, 2, own2, rest2, kk, vv)
     for qi in range(2 * ROW):
@@ -369,30 +378,33 @@
     for qi in range(2 * ROW):
         lse_ref[qi] = state[0, qi] + jnp.log(state[1, qi])
         attn_ref[qi * BLOCK : (qi + 1) * BLOCK, :] = (state[2, qi] / state[1, qi]).astype(BF16)
-    term = None
-    for d, g in enumerate((g0, g1, g2, g3)):
+    if not last:
+        return
+    total = None
+    for d, g in enumerate(gos):
         rows = g.shape[0]
-        at = pl.multiple_of((r ^ d) * rows, rows)
-        part = tn(attn_ref[pl.ds(at, rows), :], g[...])
-        term = part if term is None else term + part
-    if not last:
-        terms[0][...] = term.astype(BF16)
+        at = pl.ds(pl.multiple_of((r ^ d) * rows, rows), rows)
+        part = tn(jnp.concatenate([earlier[at, :], attn_ref[at, :]], axis=1), g[...])
+        total = part if total is None else total + part
+    if len(terms) == 1:
+        terms[0][...] = total.astype(BF16)
         return
-    wide[0:LANES, :] = earlier[...]
-    wide[LANES : 2 * LANES, :] = term.astype(BF16)
+    wide[...] = total.astype(BF16)
     half = LANES // 2
     for delta, out in enumerate(terms):
         at = pl.multiple_of((z + delta) % ROW * half, half)
         out[...] = wide[pl.ds(at, half), :]
 
 
-def far(chunk, last, lists, own2, rest2, gos, after, earlier, state, kk, vv, qq):
-    width = gos[0].shape[1]
-    weights = (
-        (jax.ShapeDtypeStruct((LANES // 2, width), BF16),) * 4
-        if last
-        else (jax.ShapeDtypeStruct((LANES, width), BF16),)
-    )
+def far(chunk, fast, lists, own2, rest2, after, state, kk, vv, qq, earlier=None, gos=()):
+    last = len(gos) > 0
+    width = gos[0].shape[1] if last else LANES
+    weights = (jax.ShapeDtypeStruct((LANES // 2, width), BF16),) * ROW
+    if not fast:
+        weights = (jax.ShapeDtypeStruct((2 * LANES, width), BF16),)
+    if not last:
+        weights = ()
+    more = (earlier, *gos) if last else ()
     return pl.pallas_call(
         functools.partial(far_kernel, chunk, last),
         out_shape=(
@@ -402,17 +414,17 @@
             jax.ShapeDtypeStruct((8, BLOCK, LANES), F32),
         )
         + weights,
-        in_specs=[SMEM] + [VMEM] * 2 + [VMEM] * ROW + [ANY, VMEM if last else ANY] + [VMEM] * 4,
+        in_specs=[SMEM] + [VMEM] * 2 + [ANY] + [VMEM] * (4 + len(more)),
         out_specs=[VMEM] * (4 + len(weights)),
-        input_output_aliases={10: 0, 11: 1},
+        input_output_aliases={5: 0, 6: 1},
         scratch_shapes=[
             pltpu.VMEM((3, 8, BLOCK, LANES), F32),
             pltpu.VMEM((2 * LANES, width), BF16),
         ],
         compiler_params=params(),
-        cost_estimate=SMALL,
+        cost_estimate=SMALL if last else micros(4.2),
         name=f"far{chunk}",
-    )(lists, own2, rest2, *gos, after, earlier, state, kk, vv, qq)
+    )(lists, own2, rest2, after, state, kk, vv, qq, *more)
 
 
 def bwd_group(kk, vv, q2, g2, lse, delta, ks, vs, diag=None):
@@ -498,7 +510,7 @@
         out_specs=[VMEM] * len(which_d),
         scratch_shapes=[pltpu.VMEM((2 * len(which_d), 2 * BLOCK, LANES), F32)],
         compiler_params=params(),
-        cost_estimate=SMALL,
+        cost_estimate=SMALL if chunk else micros(8.4),
         name=f"back{chunk}_{which_d[0]}",
     )(lists, kk, vv, qq, grads, attn, lse, after)
 
@@ -553,43 +565,48 @@
     count = lax.axis_size("span")
     fast = count == HEADS
 
-    own0, firsts = pack_first(track, keys, values)
+    own0, firsts = pack_first(keys, values)
     own1 = later(own0, "span")
     got_first = [swap(x, "span", d + 1) for d, x in enumerate(firsts)]
     queries, _ = hold((queries, got_first[0]))
-    seconds = list(pack_second(queries, keys, values))
+    seconds, turns = pack_second(track, queries, keys, values)
     got_first, _ = hold((got_first, seconds[0]))
     rest0 = [stack(2 * rows, got_first)]
     rest1 = [later(rest0[0], "span")]
+    seconds, _ = hold((seconds, (rest0[0], own1)))
+    got_second = [swap(x, "span", d + 1) for d, x in enumerate(seconds)]
     track_row = jnp.concatenate(
-        [track.astype(BF16)] + [x[2 * rows : 2 * rows + 2, : 2 * WINDOW] for x in got_first], axis=0
+        [track.astype(BF16)] + [x[2 * rows : 2 * rows + 2, : 2 * WINDOW] for x in got_second], axis=0
     )
     lists = plan(track_row.astype(jnp.int32))
 
-    seconds, _ = hold((seconds, (rest0[0], own1)))
-    seconds[1:] = [swap(seconds[d], "span", d) for d in (1, 2, 3)]
-    own2 = later(own1, "span")
-    arrived, _ = hold((seconds[1:], (rest1[0], own2, lists)))
-    rest0.append(stack(2 * rows, arrived))
+    got_second, _ = hold((got_second, rest1[0]))
+    rest0.append(stack(2 * rows, got_second))
+    turns, _ = hold((turns, (rest0[1], rest1[0])))
     rest1.append(later(rest0[1], "span"))
-    grad_late, _ = hold((grad_out, rest0[1]))
+    own1_late, _ = hold((own1, rest1[1]))
+    own2 = later(own1_late, "span")
+    turns[1:] = [swap(turns[d], "span", d) for d in (1, 2, 3)]
+    grad_late, _ = hold((grad_out, (turns, rest1[1])))
     go2 = swap(grad_late, "span", 2)
 
-    stores = [near(0, lists, own0, rest0[0], own1, rest1[0], seconds, lists)]
-    first_row, _ = hold((rest1[0], stores[0][0]))
-    rest2 = [later(first_row, "span"), later(rest1[1], "span")]
-    (grad_late, go2), _ = hold(((grad_out, go2), (stores[0][0], rest1[1])))
+    turns, _ = hold((turns, rest1[1]))
+    stores = [near(0, lists, own0, rest0[0], own1, rest1[0], turns, lists)]
+    stores.append(near(1, lists, own0, rest0[1], own1, rest1[1], turns, stores[0][0]))
+    first_row, _ = hold((rest1[0], rest1[1]))
+    (second_row, grad_late, go2), _ = hold(((rest1[1], grad_out, go2), stores[1][0]))
+    rest2 = [later(first_row, "span"), later(second_row, "span")]
     gos = (grad_out, swap(grad_late, "span", 1), go2, swap(go2, "span", 1))
     grads = grad_attn(out_weight, gos)
-    stores.append(near(1, lists, own0, rest0[1], own1, rest1[1], seconds, stores[0][0]))
 
     after = stores[1][0]
-    kk, vv, attn, lse, term = far(0, False, lists, own2, rest2[0], gos, after, after, *stores[0])
+    kk, vv, attn, lse = far(0, fast, lists, own2, rest2[0], after, *stores[0])
     out = back(0, (0, 1, 2, 3), lists, kk, vv, stores[0][3], grads, attn, lse, attn)
     pieces = [out[0]] + [swap(out[d], "span", d) for d in (1, 2, 3)]
-    grads_out = unpack(0, pieces, rows, width, ())
-
-    kk, vv, attn, lse, *terms = far(1, fast, lists, own2, rest2[1], gos, out[0], term, *stores[1])
+
+    kk, vv, attn, lse, *terms = far(
+        1, fast, lists, own2, rest2[1], out[0], *stores[1], earlier=attn, gos=gos
+    )
     second = (lists, kk, vv, stores[1][3], grads, attn, lse)
     if fast:
         weight_grad = terms[0].astype(F32)
@@ -601,12 +618,13 @@
     else:
         head_dim = width // HEADS
         place_in_row = lax.axis_index("span").astype(jnp.int32) % ROW
-        mine = jnp.concatenate([term, terms[0]], axis=0).reshape(ROW, 1, head_dim, width)
+        mine = terms[0].reshape(ROW, 1, head_dim, width)
         full = jnp.zeros((ROW, ROW, head_dim, width), BF16)
         full = lax.dynamic_update_slice(full, mine, (0, place_in_row, 0, 0)).reshape(width, width)
         weight_grad = lax.psum_scatter(full.astype(F32), "span", scatter_dimension=0, tiled=True)
     out = back(1, (1, 2, 3), *second, attn)
-    out, grads_out = hold((out, grads_out))
+    out, pieces = hold((out, pieces))
+    grads_out = unpack(0, pieces, rows, width, ())
     crossed = [swap(x, "span", d) for x, d in zip(out, (1, 2, 3))]
     (own,) = back(1, (0,), *second, out[0])
     pieces = [own] + crossed

time: 101 us -> 97.6 us (0.966)
  waiting for transfers between devices: 22.3 us -> 16 us
  starting transfers between devices: 29.3 us -> 32.3 us
  Pallas kernels: 40.1 us -> 38.9 us
    ppermute x6, waiting for transfers between devices: 12.3 us -> 4.26 us  [later(): lax.ppermute(value, axis, [(s, (s + ROW) % count) for s in range(count)])]
    ppermute x6, starting transfers between devices: 8.33 us -> 11.4 us  [later(): lax.ppermute(value, axis, [(s, (s + ROW) % count) for s in range(count)])]
    ppermute x3, waiting for transfers between devices: 0.01 us -> 2.73 us  [shards(): weight_grad += lax.ppermute(terms[delta], 'span', pairs).astype(F32)]
    ppermute x3, starting transfers between devices: 7.74 us -> 5.5 us  [shards(): weight_grad += lax.ppermute(terms[delta], 'span', pairs).astype(F32)]
    ppermute x15 -> x18, starting transfers between devices: 13.2 us -> 15.4 us  [swap(): return lax.ppermute(value, axis, [(s, s ^ bit) for s in range(count)])]
    ppermute x15 -> x18, waiting for transfers between devices: 9.93 us -> 8.99 us  [swap(): return lax.ppermute(value, axis, [(s, s ^ bit) for s in range(count)])]
    unnamed x22 -> x20, local copies, waits for them, and re-layouts: 6.59 us -> 6.64 us
  transfers between devices with their start and end apart: 24 -> 27, of which waited for: 8 -> 7; matrix products, arithmetic and copies ran while one was open for 1% -> 1% of each run, Pallas kernels for 38% -> 39%
where the time goes in v1:
time: 97.6 us; the launch traced here: 96 us
  Pallas kernels  38.9 us (40%)
  starting transfers between devices  32.3 us (33%)
  waiting for transfers between devices  16 us (16%)
  local copies, waits for them, and re-layouts  6.64 us (7%)
  other arithmetic  1.38 us (1%)
    ppermute x18, starting transfers between devices, swap(): return lax.ppermute(value, axis, [(s, s ^ bit) for s in range(count)])  15.4 us
    pallas_call x3, Pallas kernels, back(): pl.pallas_call(functools.partial(back_kernel, chunk, which_d), out_shape=...  14.9 us
    ppermute x6, starting transfers between devices, later(): lax.ppermute(value, axis, [(s, (s + ROW) % count) for s in range(count)])  11.4 us
    pallas_call x2, Pallas kernels, near(): pl.pallas_call(functools.partial(near_kernel, chunk), out_shape=(jax.Shap...  10.8 us
    ppermute x18, waiting for transfers between devices, swap(): return lax.ppermute(value, axis, [(s, s ^ bit) for s in range(count)])  8.99 us
    pallas_call x2, Pallas kernels, far(): pl.pallas_call(functools.partial(far_kernel, chunk, last), out_shape=(jax...  6.67 us
    unnamed x20, local copies, waits for them, and re-layouts  6.64 us
    ppermute x3, starting transfers between devices, shards(): weight_grad += lax.ppermute(terms[delta], 'span', pairs).astype(F32)  5.5 us
  transfers between devices with their start and end apart: 27, of which 7 were waited for; matrix products, arithmetic and copies ran while one was open for 1% of the time, Pallas kernels for 39%

profile of v1, /device:TPU:11, one launch (start us, length us, event | category | flops | bytes accessed | tf_op | source)
XLA Modules:
  0.0 96.0 jit_solution(8793918589209614989)
XLA Ops:
  0.6 0.0 copy-start.2
  0.7 1.1 %copy-done.2 = bf16[256,1024]{1,0:T(8,128)(2,1)S(1)} copy-done((bf16[256,1024]{1,0:T(8,128)(2,1)S(1)}, bf16[256,1024]{1,0:T(8,128)(2,1)}, u32[]{:S(2)}) %copy-start.2) | copy-done | bytes 524312
  1.7 1.0 %copy-done.4 = bf16[256,1024]{1,0:T(8,128)(2,1)S(1)} copy-done((bf16[256,1024]{1,0:T(8,128)(2,1)S(1)}, bf16[256,1024]{1,0:T(8,128)(2,1)}, u32[]{:S(2)}) %copy-start.4) | copy-done | bytes 524312
  2.8 0.4 pack_first.1
  3.2 0.7 collective-permute-start
  3.9 1.3 %collective-permute-start.1 = (bf16[512,128]{1,0:T(8,128)(2,1)S(1)}, bf16[512,128]{1,0:T(8,128)(2,1)S(1)}, u32[]{:S(2)}, u32[]{:S(2)}) collective-permute-start(bf16[512,128]{1,0:T(8,128)(2,1)S(1)} %get-tuple-element.84), channel_id=1, source_target_pairs={{0,2},{1,3},{2,0},{3,1},{4,6},{5,7},{6,4},{7,5},{8,10},{9,11},{10,... | collective-permute-start | bytes 393224 | tf_op jit(solution)/shard_map/ppermute | solution.py:552
  5.2 0.5 collective-permute-start.2
  5.7 1.3 %collective-permute-start.3 = (bf16[1024,128]{1,0:T(8,128)(2,1)S(1)}, bf16[1024,128]{1,0:T(8,128)(2,1)S(1)}, u32[]{:S(2)}, u32[]{:S(2)}) collective-permute-start(bf16[1024,128]{1,0:T(8,128)(2,1)S(1)} %get-tuple-element.89.own0), channel_id=1, source_target_pairs={{0,4},{1,5},{2,6},{3,7},{4,8},{5,9},{6,10},{7,11},{8,12},{9,13},{1... | collective-permute-start | bytes 786440 | tf_op jit(solution)/shard_map/ppermute | solution.py:557
  7.0 1.0 %copy-done.3 = bf16[256,1024]{1,0:T(8,128)(2,1)S(1)} copy-done((bf16[256,1024]{1,0:T(8,128)(2,1)S(1)}, bf16[256,1024]{1,0:T(8,128)(2,1)}, u32[]{:S(2)}) %copy-start.3) | copy-done | bytes 524312
  8.0 1.0 %copy-done.5 = bf16[256,1024]{1,0:T(8,128)(2,1)S(1)} copy-done((bf16[256,1024]{1,0:T(8,128)(2,1)S(1)}, bf16[256,1024]{1,0:T(8,128)(2,1)}, u32[]{:S(2)}) %copy-start.5) | copy-done | bytes 524312
  9.0 1.0 %copy-done.6 = bf16[256,1024]{1,0:T(8,128)(2,1)S(1)} copy-done((bf16[256,1024]{1,0:T(8,128)(2,1)S(1)}, bf16[256,1024]{1,0:T(8,128)(2,1)}, u32[]{:S(2)}) %copy-start.6) | copy-done | bytes 524312
  10.1 0.7 copy-done.8
  10.8 0.6 pack_second.1
  11.3 0.0 collective-permute-done.1.b
  11.4 0.9 collective-permute-done.2.c
  12.3 1.3 %collective-permute-start.7 = (bf16[1536,128]{1,0:T(8,128)(2,1)S(1)}, bf16[1536,128]{1,0:T(8,128)(2,1)S(1)}, u32[]{:S(2)}, u32[]{:S(2)}) collective-permute-start(bf16[1536,128]{1,0:T(8,128)(2,1)S(1)} %stack.2.rest0), channel_id=1, source_target_pairs={{0,4},{1,5},{2,6},{3,7},{4,8},{5,9},{6,10},{7,11},{8,12},{9,13},{1... | collective-permute-start | bytes 1179656 | tf_op jit(solution)/shard_map/ppermute | solution.py:557
  13.7 0.7 collective-permute-start.4
  14.4 1.2 %collective-permute-start.5 = (bf16[528,128]{1,0:T(8,128)(2,1)S(1)}, bf16[528,128]{1,0:T(8,128)(2,1)S(1)}, u32[]{:S(2)}, u32[]{:S(2)}) collective-permute-start(bf16[528,128]{1,0:T(8,128)(2,1)S(1)} %get-tuple-element.91), channel_id=1, source_target_pairs={{0,2},{1,3},{2,0},{3,1},{4,6},{5,7},{6,4},{7,5},{8,10},{9,11},{10,... | collective-permute-start | bytes 405512 | tf_op jit(solution)/shard_map/ppermute | solution.py:552
  15.6 0.4 collective-permute-start.6
  16.0 0.0 collective-permute-done.4.a
  16.0 3.6 %collective-permute-done.5.b = bf16[528,128]{1,0:T(8,128)(2,1)S(1)} collective-permute-done((bf16[528,128]{1,0:T(8,128)(2,1)S(1)}, bf16[528,128]{1,0:T(8,128)(2,1)S(1)}, u32[]{:S(2)}, u32[]{:S(2)}) %collective-permute-start.5) | collective-permute-done | bytes 135200 | tf_op jit(solution)/shard_map/ppermute | solution.py:552
  19.6 3.3 %collective-permute-done.6.c = bf16[528,128]{1,0:T(8,128)(2,1)S(1)} collective-permute-done((bf16[528,128]{1,0:T(8,128)(2,1)S(1)}, bf16[528,128]{1,0:T(8,128)(2,1)S(1)}, u32[]{:S(2)}, u32[]{:S(2)}) %collective-permute-start.6) | collective-permute-done | bytes 135200 | tf_op jit(solution)/shard_map/ppermute | solution.py:552
  22.9 0.3 collective-permute-done.7.rest1
  23.2 1.3 %collective-permute-start.8 = (bf16[1536,128]{1,0:T(8,128)(2,1)S(1)}, bf16[1536,128]{1,0:T(8,128)(2,1)S(1)}, u32[]{:S(2)}, u32[]{:S(2)}) collective-permute-start(bf16[1536,128]{1,0:T(8,128)(2,1)S(1)} %stack.3.rest0), channel_id=1, source_target_pairs={{0,4},{1,5},{2,6},{3,7},{4,8},{5,9},{6,10},{7,11},{8,12},{9,13},{1... | collective-permute-start | bytes 1179656 | tf_op jit(solution)/shard_map/ppermute | solution.py:557
  24.6 1.0 %collective-permute-start.10 = (bf16[512,128]{1,0:T(8,128)(2,1)S(1)}, bf16[512,128]{1,0:T(8,128)(2,1)S(1)}, u32[]{:S(2)}, u32[]{:S(2)}) collective-permute-start(bf16[512,128]{1,0:T(8,128)(2,1)S(1)} %get-tuple-element.102), channel_id=1, source_target_pairs={{0,1},{1,0},{2,3},{3,2},{4,5},{5,4},{6,7},{7,6},{8,9},{9,8},{10,11... | collective-permute-start | bytes 393224 | tf_op jit(solution)/shard_map/ppermute | solution.py:552
  25.6 1.2 %collective-permute-start.11 = (bf16[512,128]{1,0:T(8,128)(2,1)S(1)}, bf16[512,128]{1,0:T(8,128)(2,1)S(1)}, u32[]{:S(2)}, u32[]{:S(2)}) collective-permute-start(bf16[512,128]{1,0:T(8,128)(2,1)S(1)} %get-tuple-element.103), channel_id=1, source_target_pairs={{0,2},{1,3},{2,0},{3,1},{4,6},{5,7},{6,4},{7,5},{8,10},{9,11},{10,... | collective-permute-start | bytes 393224 | tf_op jit(solution)/shard_map/ppermute | solution.py:552
  26.8 0.4 collective-permute-start.12
  27.2 0.6 maximum_convert_fusion.track_ref
  27.8 2.3 %plan.1.list_ref.after = s32[8,26]{1,0:T(8,128)} custom-call(s32[8,16]{1,0:T(8,128)} %maximum_convert_fusion.track_ref), custom_call_target="tpu_custom_call" | custom-call | flops 1000000 | bytes 100000 | tf_op jit(solution)/shard_map/plan/pallas_call | solution.py:205
  30.1 3.9 %collective-permute-done.8.rest1 = bf16[1536,128]{1,0:T(8,128)(2,1)S(1)} collective-permute-done((bf16[1536,128]{1,0:T(8,128)(2,1)S(1)}, bf16[1536,128]{1,0:T(8,128)(2,1)S(1)}, u32[]{:S(2)}, u32[]{:S(2)}) %collective-permute-start.8) | collective-permute-done | bytes 393248 | tf_op jit(solution)/shard_map/ppermute | solution.py:557
  34.1 0.0 collective-permute-done.12.s3
  34.1 1.1 %collective-permute-start.9 = (bf16[1024,128]{1,0:T(8,128)(2,1)S(1)}, bf16[1024,128]{1,0:T(8,128)(2,1)S(1)}, u32[]{:S(2)}, u32[]{:S(2)}) collective-permute-start(bf16[1024,128]{1,0:T(8,128)(2,1)S(1)} %collective-permute-done.3.own1), channel_id=1, source_target_pairs={{0,4},{1,5},{2,6},{3,7},{4,8},{5,9},{6,10},{7,11},{8,12},{9,13},{1... | collective-permute-start | bytes 786440 | tf_op jit(solution)/shard_map/ppermute | solution.py:557
  35.2 1.8 %collective-permute-start.15 = (bf16[1536,128]{1,0:T(8,128)(2,1)S(1)}, bf16[1536,128]{1,0:T(8,128)(2,1)S(1)}, u32[]{:S(2)}, u32[]{:S(2)}) collective-permute-start(bf16[1536,128]{1,0:T(8,128)(2,1)S(1)} %collective-permute-done.7.rest1), channel_id=1, source_target_pairs={{0,4},{1,5},{2,6},{3,7},{4,8},{5,9},{6,10},{7,11},{8,12},{9,13},{1... | collective-permute-start | bytes 1179656 | tf_op jit(solution)/shard_map/ppermute | solution.py:557
  37.0 1.2 %collective-permute-start.13 = (bf16[256,1024]{1,0:T(8,128)(2,1)S(1)}, bf16[256,1024]{1,0:T(8,128)(2,1)S(1)}, u32[]{:S(2)}, u32[]{:S(2)}) collective-permute-start(bf16[256,1024]{1,0:T(8,128)(2,1)S(1)} %copy-done), channel_id=1, source_target_pairs={{0,2},{1,3},{2,0},{3,1},{4,6},{5,7},{6,4},{7,5},{8,10},{9,11},{10,... | collective-permute-start | bytes 1572872 | tf_op jit(solution)/shard_map/ppermute | solution.py:552
  38.2 0.7 copy-done.7
  38.9 5.4 %near0.1 = (f32[3,8,128,128]{3,2,1,0:T(8,128)S(1)}, bf16[29,128,128]{2,1,0:T(8,128)(2,1)S(1)}, bf16[29,128,256]{2,1,0:T(8,128)(2,1)S(1)}, bf16[8,128,128]{2,1,0:T(8,128)(2,1)S(1)}) custom-call(s32[8,26]{1,0:T(8,128)S(1)} %copy-done.7, bf16[1024,128]{1,0:T(8,128)(2,1)S(1)} %get-tuple-element.89.own0, bf16[1536,128]{1,0:T(8,128)(2,1)S(1)} %stack.2.rest0, ...), custom_call_target="tpu_custom_call" | custom-call | flops 6049999872 | bytes 100000 | tf_op jit(solution)/shard_map/near0/pallas_call | solution.py:330
  44.3 5.4 %near1.1 = (f32[3,8,128,128]{3,2,1,0:T(8,128)S(1)}, bf16[29,128,128]{2,1,0:T(8,128)(2,1)S(1)}, bf16[29,128,256]{2,1,0:T(8,128)(2,1)S(1)}, bf16[8,128,128]{2,1,0:T(8,128)(2,1)S(1)}) custom-call(s32[8,26]{1,0:T(8,128)S(1)} %copy-done.7, bf16[1024,128]{1,0:T(8,128)(2,1)S(1)} %get-tuple-element.89.own0, bf16[1536,128]{1,0:T(8,128)(2,1)S(1)} %stack.3.rest0, ...), custom_call_target="tpu_custom_call" | custom-call | flops 1000000 | bytes 100000 | tf_op jit(solution)/shard_map/near1/pallas_call | solution.py:330
  49.8 0.0 collective-permute-done.13.g2.refs_3_
  49.8 1.6 %collective-permute-start.16 = (bf16[256,1024]{1,0:T(8,128)(2,1)S(1)}, bf16[256,1024]{1,0:T(8,128)(2,1)S(1)}, u32[]{:S(2)}, u32[]{:S(2)}) collective-permute-start(bf16[256,1024]{1,0:T(8,128)(2,1)S(1)} %copy-done), channel_id=1, source_target_pairs={{0,1},{1,0},{2,3},{3,2},{4,5},{5,4},{6,7},{7,6},{8,9},{9,8},{10,11... | collective-permute-start | bytes 1572872 | tf_op jit(solution)/shard_map/ppermute | solution.py:552
  51.3 0.0 collective-permute-start.17
  51.3 0.0 copy-start.1
  51.4 2.9 %far0.1 = (bf16[29,128,128]{2,1,0:T(8,128)(2,1)S(1)}, bf16[29,128,256]{2,1,0:T(8,128)(2,1)S(1)}, bf16[1024,128]{1,0:T(8,128)(2,1)S(1)}, f32[8,128,128]{2,1,0:T(8,128)S(1)}) custom-call(s32[8,26]{1,0:T(8,128)S(1)} %copy-done.7, bf16[1024,128]{1,0:T(8,128)(2,1)S(1)} %collective-permute-done.9.own2, ...), custom_call_target="tpu_custom_call", output_to_operand_aliasing={{0}: (5, {}), {1}: (6, {})} | custom-call | flops 4620000256 | bytes 100000 | tf_op jit(solution)/shard_map/far0/pallas_call | solution.py:408
  54.3 4.5 %collective-permute-start.14 = (bf16[1536,128]{1,0:T(8,128)(2,1)S(1)}, bf16[1536,128]{1,0:T(8,128)(2,1)S(1)}, u32[]{:S(2)}, u32[]{:S(2)}) collective-permute-start(bf16[1536,128]{1,0:T(8,128)(2,1)S(1)} %collective-permute-done.8.rest1), channel_id=1, source_target_pairs={{0,4},{1,5},{2,6},{3,7},{4,8},{5,9},{6,10},{7,11},{8,12},{9,13},{1... | collective-permute-start | bytes 1179656 | tf_op jit(solution)/shard_map/ppermute | solution.py:557
  58.8 0.0 collective-permute-done.16.g1.refs_2_
  58.8 0.0 collective-permute-done.17.g3.refs_4_
  58.8 0.8 grad_attn.1.g_ref
  59.6 7.1 %back0_0.1 = (bf16[768,128]{1,0:T(8,128)(2,1)S(1)}, bf16[768,128]{1,0:T(8,128)(2,1)S(1)}, bf16[768,128]{1,0:T(8,128)(2,1)S(1)}, bf16[768,128]{1,0:T(8,128)(2,1)S(1)}) custom-call(s32[8,26]{1,0:T(8,128)S(1)} %copy-done.7, bf16[29,128,128]{2,1,0:T(8,128)(2,1)S(1)} %get-tuple-element.117.kk, bf16[29,128,256]{2,1,0:T(8,128)(2,1)S(1)} %get-tuple-element.118.vv, ...), custom_call_target="tpu_custom_call" | custom-call | flops 9240000512 | bytes 100000 | tf_op jit(solution)/shard_map/back0_0/pallas_call | solution.py:506
  66.7 0.8 collective-permute-start.18
  67.5 0.3 collective-permute-start.19
  67.8 1.4 %collective-permute-start.20 = (bf16[768,128]{1,0:T(8,128)(2,1)S(1)}, bf16[768,128]{1,0:T(8,128)(2,1)S(1)}, u32[]{:S(2)}, u32[]{:S(2)}) collective-permute-start(bf16[768,128]{1,0:T(8,128)(2,1)S(1)} %get-tuple-element.136), channel_id=1, source_target_pairs={{0,3},{1,2},{2,1},{3,0},{4,7},{5,6},{6,5},{7,4},{8,11},{9,10},{10,... | collective-permute-start | bytes 589832 | tf_op jit(solution)/shard_map/ppermute | solution.py:552
  69.2 0.0 collective-permute-done.14.rest2
  69.2 3.7 %far1.1 = (bf16[29,128,128]{2,1,0:T(8,128)(2,1)S(1)}, bf16[29,128,256]{2,1,0:T(8,128)(2,1)S(1)}, bf16[1024,128]{1,0:T(8,128)(2,1)S(1)}, f32[8,128,128]{2,1,0:T(8...) custom-call(s32[8,26]{1,0:T(8,128)S(1)} %copy-done.7, ...), custom_call_target="tpu_custom_call", output_to_operand_aliasing={{0}: (5, {}), {1}: (6, {})} | custom-call | flops 1000000 | bytes 100000 | tf_op jit(solution)/shard_map/far1/pallas_call | solution.py:408
  72.9 0.7 collective-permute-start.24
  73.6 3.4 %collective-permute-start.25 = (bf16[64,1024]{1,0:T(8,128)(2,1)S(1)}, bf16[64,1024]{1,0:T(8,128)(2,1)S(1)}, u32[]{:S(2)}, u32[]{:S(2)}) collective-permute-start(bf16[64,1024]{1,0:T(8,128)(2,1)S(1)} %get-tuple-element.152), channel_id=1, source_target_pairs={{0,8},{1,9},{2,10},{3,11},{4,12},{5,13},{6,14},{7,15},{8,0},{9,1},... | collective-permute-start | bytes 393224 | tf_op jit(solution)/shard_map/ppermute | solution.py:617
  77.0 1.4 %collective-permute-start.26 = (bf16[64,1024]{1,0:T(8,128)(2,1)S(1)}, bf16[64,1024]{1,0:T(8,128)(2,1)S(1)}, u32[]{:S(2)}, u32[]{:S(2)}) collective-permute-start(bf16[64,1024]{1,0:T(8,128)(2,1)S(1)} %get-tuple-element.153), channel_id=1, source_target_pairs={{0,12},{1,13},{2,14},{3,15},{4,0},{5,1},{6,2},{7,3},{8,4},{9,5},{1... | collective-permute-start | bytes 393224 | tf_op jit(solution)/shard_map/ppermute | solution.py:617
  78.4 5.5 %back1_1.1 = (bf16[768,128]{1,0:T(8,128)(2,1)S(1)}, bf16[768,128]{1,0:T(8,128)(2,1)S(1)}, bf16[768,128]{1,0:T(8,128)(2,1)S(1)}) custom-call(s32[8,26]{1,0:T(8,128)S(1)} %copy-done.7, bf16[29,128,128]{2,1,0:T(8,128)(2,1)S(1)} %get-tuple-element.127.kk, bf16[29,128,256]{2,1,0:T(8,128)(2,1)S(1)} %get-tuple-element.128.vv, ...), custom_call_target="tpu_custom_call" | custom-call | flops 1000000 | bytes 100000 | tf_op jit(solution)/shard_map/back1_1/pallas_call | solution.py:506
  83.9 1.3 %collective-permute-start.22 = (bf16[768,128]{1,0:T(8,128)(2,1)S(1)}, bf16[768,128]{1,0:T(8,128)(2,1)S(1)}, u32[]{:S(2)}, u32[]{:S(2)}) collective-permute-start(bf16[768,128]{1,0:T(8,128)(2,1)S(1)} %get-tuple-element.138), channel_id=1, source_target_pairs={{0,2},{1,3},{2,0},{3,1},{4,6},{5,7},{6,4},{7,5},{8,10},{9,11},{10,... | collective-permute-start | bytes 589832 | tf_op jit(solution)/shard_map/ppermute | solution.py:552
  85.3 1.4 %collective-permute-start.23 = (bf16[768,128]{1,0:T(8,128)(2,1)S(1)}, bf16[768,128]{1,0:T(8,128)(2,1)S(1)}, u32[]{:S(2)}, u32[]{:S(2)}) collective-permute-start(bf16[768,128]{1,0:T(8,128)(2,1)S(1)} %get-tuple-element.139), channel_id=1, source_target_pairs={{0,3},{1,2},{2,1},{3,0},{4,7},{5,6},{6,5},{7,4},{8,11},{9,10},{10,... | collective-permute-start | bytes 589832 | tf_op jit(solution)/shard_map/ppermute | solution.py:552
  86.6 2.7 %collective-permute-done.26 = bf16[64,1024]{1,0:T(8,128)(2,1)S(1)} collective-permute-done((bf16[64,1024]{1,0:T(8,128)(2,1)S(1)}, bf16[64,1024]{1,0:T(8,128)(2,1)S(1)}, u32[]{:S(2)}, u32[]{:S(2)}) %collective-permute-start.26) | collective-permute-done | bytes 131104 | tf_op jit(solution)/shard_map/ppermute | solution.py:617
  89.4 0.8 convert_add_fusion
  90.1 2.3 %back1_0.1.refs_0_ = bf16[768,128]{1,0:T(8,128)(2,1)S(1)} custom-call(s32[8,26]{1,0:T(8,128)S(1)} %copy-done.7, bf16[29,128,128]{2,1,0:T(8,128)(2,1)S(1)} %get-tuple-element.127.kk, bf16[29,128,256]{2,1,0:T(8,128)(2,1)S(1)} %get-tuple-element.128.vv, bf16[8,128,128]{2,1,0:T(8,128)(2,1)S(1)} %get-tuple-element.126.qq, bf16[1024,256]{1,0:T(8,128)(2,1)S(1)} %grad_attn.1.g_ref, ...), custom_call_target="tpu_custom_call" | custom-call | flops 1000000 | bytes 100000 | tf_op jit(solution)/shard_map/back1_0/pallas_call | solution.py:506
  92.5 1.2 %unpack0.1 = (bf16[256,1024]{1,0:T(8,128)(2,1)}, bf16[256,1024]{1,0:T(8,128)(2,1)}, bf16[256,1024]{1,0:T(8,128)(2,1)}) custom-call(bf16[768,128]{1,0:T(8,128)(2,1)S(1)} %get-tuple-element.140.after.refs_0_, bf16[768,128]{1,0:T(8,128)(2,1)S(1)} %collective-permute-done.18.refs_1_, bf16[768,128]{1,0:T(8,128)(2,1)S(1)} %collective-permute-done.19.refs_2_, ...), custom_call_target="tpu_custom_call" | custom-call | flops 1000000 | bytes 100000 | tf_op jit(solution)/shard_map/unpack0/pallas_call | solution.py:537
  93.7 1.2 %collective-permute-done.23.refs_3_ = bf16[768,128]{1,0:T(8,128)(2,1)S(1)} collective-permute-done((bf16[768,128]{1,0:T(8,128)(2,1)S(1)}, bf16[768,128]{1,0:T(8,128)(2,1)S(1)}, u32[]{:S(2)}, u32[]{:S(2)}) %collective-permute-start.23) | collective-permute-done | bytes 196640 | tf_op jit(solution)/shard_map/ppermute | solution.py:552
  94.8 1.2 %unpack1.1 = (bf16[256,1024]{1,0:T(8,128)(2,1)}, bf16[256,1024]{1,0:T(8,128)(2,1)}, bf16[256,1024]{1,0:T(8,128)(2,1)}) custom-call(bf16[768,128]{1,0:T(8,128)(2,1)S(1)} %back1_0.1.refs_0_, bf16[768,128]{1,0:T(8,128)(2,1)S(1)} %collective-permute-done.21.refs_1_, ...), custom_call_target="tpu_custom_call", output_to_operand_aliasing={{0}: (4, {}), {1}: (5, {}), {2}: (6, {})} | custom-call | flops 1000000 | bytes 100000 | tf_op jit(solution)/shard_map/unpack1/pallas_call | solution.py:537
  (31 shorter events, 0.1 us)
Async XLA Ops:
  0.6 36.4 %copy-start = (bf16[256,1024]{1,0:T(8,128)(2,1)S(1)}, bf16[256,1024]{1,0:T(8,128)(2,1)}, u32[]{:S(2)}) copy-start(bf16[256,1024]{1,0:T(8,128)(2,1)} %refs_1_.1) | copy-start | bytes 1572868
  0.6 1.1 %copy-start.2 = (bf16[256,1024]{1,0:T(8,128)(2,1)S(1)}, bf16[256,1024]{1,0:T(8,128)(2,1)}, u32[]{:S(2)}) copy-start(bf16[256,1024]{1,0:T(8,128)(2,1)} %k_ref.1) | copy-start | bytes 1572868
  1.7 1.0 %copy-start.4 = (bf16[256,1024]{1,0:T(8,128)(2,1)S(1)}, bf16[256,1024]{1,0:T(8,128)(2,1)}, u32[]{:S(2)}) copy-start(bf16[256,1024]{1,0:T(8,128)(2,1)} %v_ref.1) | copy-start | bytes 1572868
  2.8 24.4 %copy-start.9 = (s32[2,16]{1,0:T(2,128)S(1)}, s32[2,16]{1,0:T(2,128)}, u32[]{:S(2)}) copy-start(s32[2,16]{1,0:T(2,128)} %t_ref.1) | copy-start | bytes 388
  3.2 3.8 %collective-permute-start = (bf16[512,128]{1,0:T(8,128)(2,1)S(1)}, bf16[512,128]{1,0:T(8,128)(2,1)S(1)}, u32[]{:S(2)}, u32[]{:S(2)}) collective-permute-start(bf16[512,128]{1,0:T(8,128)(2,1)S(1)} %get-tuple-element.79), channel_id=1, source_target_pairs={{0,1},{1,0},{2,3},{3,2},{4,5},{5,4},{6,7},{7,6},{8,9},{9,8},{10,11... | collective-permute-start | bytes 393224 | tf_op jit(solution)/shard_map/ppermute | solution.py:552
  3.9 7.4 %collective-permute-start.1 = (bf16[512,128]{1,0:T(8,128)(2,1)S(1)}, bf16[512,128]{1,0:T(8,128)(2,1)S(1)}, u32[]{:S(2)}, u32[]{:S(2)}) collective-permute-start(bf16[512,128]{1,0:T(8,128)(2,1)S(1)} %get-tuple-element.84), channel_id=1, source_target_pairs={{0,2},{1,3},{2,0},{3,1},{4,6},{5,7},{6,4},{7,5},{8,10},{9,11},{10,... | collective-permute-start | bytes 393224 | tf_op jit(solution)/shard_map/ppermute | solution.py:552
  5.2 7.1 %collective-permute-start.2 = (bf16[512,128]{1,0:T(8,128)(2,1)S(1)}, bf16[512,128]{1,0:T(8,128)(2,1)S(1)}, u32[]{:S(2)}, u32[]{:S(2)}) collective-permute-start(bf16[512,128]{1,0:T(8,128)(2,1)S(1)} %get-tuple-element.85), channel_id=1, source_target_pairs={{0,3},{1,2},{2,1},{3,0},{4,7},{5,6},{6,5},{7,4},{8,11},{9,10},{10,... | collective-permute-start | bytes 393224 | tf_op jit(solution)/shard_map/ppermute | solution.py:552
  5.7 8.0 %collective-permute-start.3 = (bf16[1024,128]{1,0:T(8,128)(2,1)S(1)}, bf16[1024,128]{1,0:T(8,128)(2,1)S(1)}, u32[]{:S(2)}, u32[]{:S(2)}) collective-permute-start(bf16[1024,128]{1,0:T(8,128)(2,1)S(1)} %get-tuple-element.89.own0), channel_id=1, source_target_pairs={{0,4},{1,5},{2,6},{3,7},{4,8},{5,9},{6,10},{7,11},{8,12},{9,13},{1... | collective-permute-start | bytes 786440 | tf_op jit(solution)/shard_map/ppermute | solution.py:557
  7.0 1.0 %copy-start.3 = (bf16[256,1024]{1,0:T(8,128)(2,1)S(1)}, bf16[256,1024]{1,0:T(8,128)(2,1)}, u32[]{:S(2)}) copy-start(bf16[256,1024]{1,0:T(8,128)(2,1)} %k_ref.1) | copy-start | bytes 1572868
  8.0 1.0 %copy-start.5 = (bf16[256,1024]{1,0:T(8,128)(2,1)S(1)}, bf16[256,1024]{1,0:T(8,128)(2,1)}, u32[]{:S(2)}) copy-start(bf16[256,1024]{1,0:T(8,128)(2,1)} %v_ref.1) | copy-start | bytes 1572868
  9.0 1.0 %copy-start.6 = (bf16[256,1024]{1,0:T(8,128)(2,1)S(1)}, bf16[256,1024]{1,0:T(8,128)(2,1)}, u32[]{:S(2)}) copy-start(bf16[256,1024]{1,0:T(8,128)(2,1)} %q_ref) | copy-start | bytes 1572868
  10.1 0.7 copy-start.8
  12.3 10.9 %collective-permute-start.7 = (bf16[1536,128]{1,0:T(8,128)(2,1)S(1)}, bf16[1536,128]{1,0:T(8,128)(2,1)S(1)}, u32[]{:S(2)}, u32[]{:S(2)}) collective-permute-start(bf16[1536,128]{1,0:T(8,128)(2,1)S(1)} %stack.2.rest0), channel_id=1, source_target_pairs={{0,4},{1,5},{2,6},{3,7},{4,8},{5,9},{6,10},{7,11},{8,12},{9,13},{1... | collective-permute-start | bytes 1179656 | tf_op jit(solution)/shard_map/ppermute | solution.py:557
  13.7 2.3 %collective-permute-start.4 = (bf16[528,128]{1,0:T(8,128)(2,1)S(1)}, bf16[528,128]{1,0:T(8,128)(2,1)S(1)}, u32[]{:S(2)}, u32[]{:S(2)}) collective-permute-start(bf16[528,128]{1,0:T(8,128)(2,1)S(1)} %get-tuple-element.90), channel_id=1, source_target_pairs={{0,1},{1,0},{2,3},{3,2},{4,5},{5,4},{6,7},{7,6},{8,9},{9,8},{10,11... | collective-permute-start | bytes 405512 | tf_op jit(solution)/shard_map/ppermute | solution.py:552
  14.4 5.2 %collective-permute-start.5 = (bf16[528,128]{1,0:T(8,128)(2,1)S(1)}, bf16[528,128]{1,0:T(8,128)(2,1)S(1)}, u32[]{:S(2)}, u32[]{:S(2)}) collective-permute-start(bf16[528,128]{1,0:T(8,128)(2,1)S(1)} %get-tuple-element.91), channel_id=1, source_target_pairs={{0,2},{1,3},{2,0},{3,1},{4,6},{5,7},{6,4},{7,5},{8,10},{9,11},{10,... | collective-permute-start | bytes 405512 | tf_op jit(solution)/shard_map/ppermute | solution.py:552
  15.6 7.3 %collective-permute-start.6 = (bf16[528,128]{1,0:T(8,128)(2,1)S(1)}, bf16[528,128]{1,0:T(8,128)(2,1)S(1)}, u32[]{:S(2)}, u32[]{:S(2)}) collective-permute-start(bf16[528,128]{1,0:T(8,128)(2,1)S(1)} %get-tuple-element.92), channel_id=1, source_target_pairs={{0,3},{1,2},{2,1},{3,0},{4,7},{5,6},{6,5},{7,4},{8,11},{9,10},{10,... | collective-permute-start | bytes 405512 | tf_op jit(solution)/shard_map/ppermute | solution.py:552
  23.2 10.8 %collective-permute-start.8 = (bf16[1536,128]{1,0:T(8,128)(2,1)S(1)}, bf16[1536,128]{1,0:T(8,128)(2,1)S(1)}, u32[]{:S(2)}, u32[]{:S(2)}) collective-permute-start(bf16[1536,128]{1,0:T(8,128)(2,1)S(1)} %stack.3.rest0), channel_id=1, source_target_pairs={{0,4},{1,5},{2,6},{3,7},{4,8},{5,9},{6,10},{7,11},{8,12},{9,13},{1... | collective-permute-start | bytes 1179656 | tf_op jit(solution)/shard_map/ppermute | solution.py:557
  24.6 9.5 %collective-permute-start.10 = (bf16[512,128]{1,0:T(8,128)(2,1)S(1)}, bf16[512,128]{1,0:T(8,128)(2,1)S(1)}, u32[]{:S(2)}, u32[]{:S(2)}) collective-permute-start(bf16[512,128]{1,0:T(8,128)(2,1)S(1)} %get-tuple-element.102), channel_id=1, source_target_pairs={{0,1},{1,0},{2,3},{3,2},{4,5},{5,4},{6,7},{7,6},{8,9},{9,8},{10,11... | collective-permute-start | bytes 393224 | tf_op jit(solution)/shard_map/ppermute | solution.py:552
  25.6 8.5 %collective-permute-start.11 = (bf16[512,128]{1,0:T(8,128)(2,1)S(1)}, bf16[512,128]{1,0:T(8,128)(2,1)S(1)}, u32[]{:S(2)}, u32[]{:S(2)}) collective-permute-start(bf16[512,128]{1,0:T(8,128)(2,1)S(1)} %get-tuple-element.103), channel_id=1, source_target_pairs={{0,2},{1,3},{2,0},{3,1},{4,6},{5,7},{6,4},{7,5},{8,10},{9,11},{10,... | collective-permute-start | bytes 393224 | tf_op jit(solution)/shard_map/ppermute | solution.py:552
  26.8 7.3 %collective-permute-start.12 = (bf16[512,128]{1,0:T(8,128)(2,1)S(1)}, bf16[512,128]{1,0:T(8,128)(2,1)S(1)}, u32[]{:S(2)}, u32[]{:S(2)}) collective-permute-start(bf16[512,128]{1,0:T(8,128)(2,1)S(1)} %get-tuple-element.104), channel_id=1, source_target_pairs={{0,3},{1,2},{2,1},{3,0},{4,7},{5,6},{6,5},{7,4},{8,11},{9,10},{10,... | collective-permute-start | bytes 393224 | tf_op jit(solution)/shard_map/ppermute | solution.py:552
  34.1 17.3 %collective-permute-start.9 = (bf16[1024,128]{1,0:T(8,128)(2,1)S(1)}, bf16[1024,128]{1,0:T(8,128)(2,1)S(1)}, u32[]{:S(2)}, u32[]{:S(2)}) collective-permute-start(bf16[1024,128]{1,0:T(8,128)(2,1)S(1)} %collective-permute-done.3.own1), channel_id=1, source_target_pairs={{0,4},{1,5},{2,6},{3,7},{4,8},{5,9},{6,10},{7,11},{8,12},{9,13},{1... | collective-permute-start | bytes 786440 | tf_op jit(solution)/shard_map/ppermute | solution.py:557
  35.2 16.2 %collective-permute-start.15 = (bf16[1536,128]{1,0:T(8,128)(2,1)S(1)}, bf16[1536,128]{1,0:T(8,128)(2,1)S(1)}, u32[]{:S(2)}, u32[]{:S(2)}) collective-permute-start(bf16[1536,128]{1,0:T(8,128)(2,1)S(1)} %collective-permute-done.7.rest1), channel_id=1, source_target_pairs={{0,4},{1,5},{2,6},{3,7},{4,8},{5,9},{6,10},{7,11},{8,12},{9,13},{1... | collective-permute-start | bytes 1179656 | tf_op jit(solution)/shard_map/ppermute | solution.py:557
  37.0 12.8 %collective-permute-start.13 = (bf16[256,1024]{1,0:T(8,128)(2,1)S(1)}, bf16[256,1024]{1,0:T(8,128)(2,1)S(1)}, u32[]{:S(2)}, u32[]{:S(2)}) collective-permute-start(bf16[256,1024]{1,0:T(8,128)(2,1)S(1)} %copy-done), channel_id=1, source_target_pairs={{0,2},{1,3},{2,0},{3,1},{4,6},{5,7},{6,4},{7,5},{8,10},{9,11},{10,... | collective-permute-start | bytes 1572872 | tf_op jit(solution)/shard_map/ppermute | solution.py:552
  38.2 0.7 copy-start.7
  49.8 9.0 %collective-permute-start.16 = (bf16[256,1024]{1,0:T(8,128)(2,1)S(1)}, bf16[256,1024]{1,0:T(8,128)(2,1)S(1)}, u32[]{:S(2)}, u32[]{:S(2)}) collective-permute-start(bf16[256,1024]{1,0:T(8,128)(2,1)S(1)} %copy-done), channel_id=1, source_target_pairs={{0,1},{1,0},{2,3},{3,2},{4,5},{5,4},{6,7},{7,6},{8,9},{9,8},{10,11... | collective-permute-start | bytes 1572872 | tf_op jit(solution)/shard_map/ppermute | solution.py:552
  51.3 7.5 %collective-permute-start.17 = (bf16[256,1024]{1,0:T(8,128)(2,1)S(1)}, bf16[256,1024]{1,0:T(8,128)(2,1)S(1)}, u32[]{:S(2)}, u32[]{:S(2)}) collective-permute-start(bf16[256,1024]{1,0:T(8,128)(2,1)S(1)} %collective-permute-done.13.g2.refs_3_), channel_id=1, source_target_pairs={{0,1},{1,0},{2,3},{3,2},{4,5},{5,4},{6,7},{7,6},{8,9},{9,8},{10,11... | collective-permute-start | bytes 1572872 | tf_op jit(solution)/shard_map/ppermute | solution.py:552
  51.3 7.5 %copy-start.1 = (bf16[1024,1024]{1,0:T(8,128)(2,1)S(1)}, bf16[1024,1024]{1,0:T(8,128)(2,1)}, u32[]{:S(2)}) copy-start(bf16[1024,1024]{1,0:T(8,128)(2,1)} %w.1) | copy-start | bytes 6291460
  54.3 14.9 %collective-permute-start.14 = (bf16[1536,128]{1,0:T(8,128)(2,1)S(1)}, bf16[1536,128]{1,0:T(8,128)(2,1)S(1)}, u32[]{:S(2)}, u32[]{:S(2)}) collective-permute-start(bf16[1536,128]{1,0:T(8,128)(2,1)S(1)} %collective-permute-done.8.rest1), channel_id=1, source_target_pairs={{0,4},{1,5},{2,6},{3,7},{4,8},{5,9},{6,10},{7,11},{8,12},{9,13},{1... | collective-permute-start | bytes 1179656 | tf_op jit(solution)/shard_map/ppermute | solution.py:557
  66.7 10.3 %collective-permute-start.18 = (bf16[768,128]{1,0:T(8,128)(2,1)S(1)}, bf16[768,128]{1,0:T(8,128)(2,1)S(1)}, u32[]{:S(2)}, u32[]{:S(2)}) collective-permute-start(bf16[768,128]{1,0:T(8,128)(2,1)S(1)} %get-tuple-element.134), channel_id=1, source_target_pairs={{0,1},{1,0},{2,3},{3,2},{4,5},{5,4},{6,7},{7,6},{8,9},{9,8},{10,11... | collective-permute-start | bytes 589832 | tf_op jit(solution)/shard_map/ppermute | solution.py:552
  67.5 16.4 %collective-permute-start.19 = (bf16[768,128]{1,0:T(8,128)(2,1)S(1)}, bf16[768,128]{1,0:T(8,128)(2,1)S(1)}, u32[]{:S(2)}, u32[]{:S(2)}) collective-permute-start(bf16[768,128]{1,0:T(8,128)(2,1)S(1)} %get-tuple-element.135), channel_id=1, source_target_pairs={{0,2},{1,3},{2,0},{3,1},{4,6},{5,7},{6,4},{7,5},{8,10},{9,11},{10,... | collective-permute-start | bytes 589832 | tf_op jit(solution)/shard_map/ppermute | solution.py:552
  67.8 16.2 %collective-permute-start.20 = (bf16[768,128]{1,0:T(8,128)(2,1)S(1)}, bf16[768,128]{1,0:T(8,128)(2,1)S(1)}, u32[]{:S(2)}, u32[]{:S(2)}) collective-permute-start(bf16[768,128]{1,0:T(8,128)(2,1)S(1)} %get-tuple-element.136), channel_id=1, source_target_pairs={{0,3},{1,2},{2,1},{3,0},{4,7},{5,6},{6,5},{7,4},{8,11},{9,10},{10,... | collective-permute-start | bytes 589832 | tf_op jit(solution)/shard_map/ppermute | solution.py:552
  72.9 13.7 %collective-permute-start.24 = (bf16[64,1024]{1,0:T(8,128)(2,1)S(1)}, bf16[64,1024]{1,0:T(8,128)(2,1)S(1)}, u32[]{:S(2)}, u32[]{:S(2)}) collective-permute-start(bf16[64,1024]{1,0:T(8,128)(2,1)S(1)} %get-tuple-element.151), channel_id=1, source_target_pairs={{0,4},{1,5},{2,6},{3,7},{4,8},{5,9},{6,10},{7,11},{8,12},{9,13},{1... | collective-permute-start | bytes 393224 | tf_op jit(solution)/shard_map/ppermute | solution.py:617
  73.6 13.0 %collective-permute-start.25 = (bf16[64,1024]{1,0:T(8,128)(2,1)S(1)}, bf16[64,1024]{1,0:T(8,128)(2,1)S(1)}, u32[]{:S(2)}, u32[]{:S(2)}) collective-permute-start(bf16[64,1024]{1,0:T(8,128)(2,1)S(1)} %get-tuple-element.152), channel_id=1, source_target_pairs={{0,8},{1,9},{2,10},{3,11},{4,12},{5,13},{6,14},{7,15},{8,0},{9,1},... | collective-permute-start | bytes 393224 | tf_op jit(solution)/shard_map/ppermute | solution.py:617
  77.0 12.3 %collective-permute-start.26 = (bf16[64,1024]{1,0:T(8,128)(2,1)S(1)}, bf16[64,1024]{1,0:T(8,128)(2,1)S(1)}, u32[]{:S(2)}, u32[]{:S(2)}) collective-permute-start(bf16[64,1024]{1,0:T(8,128)(2,1)S(1)} %get-tuple-element.153), channel_id=1, source_target_pairs={{0,12},{1,13},{2,14},{3,15},{4,0},{5,1},{6,2},{7,3},{8,4},{9,5},{1... | collective-permute-start | bytes 393224 | tf_op jit(solution)/shard_map/ppermute | solution.py:617
  83.9 9.7 %collective-permute-start.22 = (bf16[768,128]{1,0:T(8,128)(2,1)S(1)}, bf16[768,128]{1,0:T(8,128)(2,1)S(1)}, u32[]{:S(2)}, u32[]{:S(2)}) collective-permute-start(bf16[768,128]{1,0:T(8,128)(2,1)S(1)} %get-tuple-element.138), channel_id=1, source_target_pairs={{0,2},{1,3},{2,0},{3,1},{4,6},{5,7},{6,4},{7,5},{8,10},{9,11},{10,... | collective-permute-start | bytes 589832 | tf_op jit(solution)/shard_map/ppermute | solution.py:552
  85.3 9.6 %collective-permute-start.23 = (bf16[768,128]{1,0:T(8,128)(2,1)S(1)}, bf16[768,128]{1,0:T(8,128)(2,1)S(1)}, u32[]{:S(2)}, u32[]{:S(2)}) collective-permute-start(bf16[768,128]{1,0:T(8,128)(2,1)S(1)} %get-tuple-element.139), channel_id=1, source_target_pairs={{0,3},{1,2},{2,1},{3,0},{4,7},{5,6},{6,5},{7,4},{8,11},{9,10},{10,... | collective-permute-start | bytes 589832 | tf_op jit(solution)/shard_map/ppermute | solution.py:552
  86.6 8.2 %collective-permute-start.21 = (bf16[768,128]{1,0:T(8,128)(2,1)S(1)}, bf16[768,128]{1,0:T(8,128)(2,1)S(1)}, u32[]{:S(2)}, u32[]{:S(2)}) collective-permute-start(bf16[768,128]{1,0:T(8,128)(2,1)S(1)} %get-tuple-element.137.after), channel_id=1, source_target_pairs={{0,1},{1,0},{2,3},{3,2},{4,5},{5,4},{6,7},{7,6},{8,9},{9,8},{10,11... | collective-permute-start | bytes 589832 | tf_op jit(solution)/shard_map/ppermute | solution.py:552

commit v2 on v1

--- a/solution.py
+++ b/solution.py
@@ -622,12 +622,14 @@
         full = jnp.zeros((ROW, ROW, head_dim, width), BF16)
         full = lax.dynamic_update_slice(full, mine, (0, place_in_row, 0, 0)).reshape(width, width)
         weight_grad = lax.psum_scatter(full.astype(F32), "span", scatter_dimension=0, tiled=True)
-    out = back(1, (1, 2, 3), *second, attn)
+    out = back(1, (2, 3), *second, attn)
     out, pieces = hold((out, pieces))
     grads_out = unpack(0, pieces, rows, width, ())
-    crossed = [swap(x, "span", d) for x, d in zip(out, (1, 2, 3))]
-    (own,) = back(1, (0,), *second, out[0])
-    pieces = [own] + crossed
+    crossed = [swap(x, "span", d) for x, d in zip(out, (2, 3))]
+    (beside,) = back(1, (1,), *second, out[0])
+    beside = swap(beside, "span", 1)
+    (own,) = back(1, (0,), *second, out[1])
+    pieces = [own, beside] + crossed
     query_grad, key_grad, value_grad = unpack(1, pieces, rows, width, grads_out)
     return (query_grad, key_grad, value_grad, weight_grad)
 

time: 97.6 us -> 96.3 us (0.987); the launches traced: 96 us -> 95.9 us
  Pallas kernels: 38.9 us -> 41.2 us
  waiting for transfers between devices: 16 us -> 14.2 us
    pallas_call x2, Pallas kernels: 10.8 us -> 12.3 us  [near(): pl.pallas_call(functools.partial(near_kernel, chunk), out_shape=(jax.Shap...]
    ppermute x6, starting transfers between devices: 11.4 us -> 10 us  [later(): lax.ppermute(value, axis, [(s, (s + ROW) % count) for s in range(count)])]
    pallas_call x3 -> x4, Pallas kernels: 14.9 us -> 15.7 us  [back(): pl.pallas_call(functools.partial(back_kernel, chunk, which_d), out_shape=...]
    unnamed x20 -> x22, local copies, waits for them, and re-layouts: 6.64 us -> 6.64 us
  transfers between devices with their start and end apart: 27 -> 27, of which waited for: 7 -> 7; matrix products, arithmetic and copies ran while one was open for 1% -> 1% of each run, Pallas kernels for 39% -> 41%
where the time goes in v2:
time: 96.3 us; the launch traced here: 95.9 us
  Pallas kernels  41.2 us (43%)
  starting transfers between devices  31.7 us (33%)
  waiting for transfers between devices  14.2 us (15%)
  local copies, waits for them, and re-layouts  6.65 us (7%)
  other arithmetic  1.38 us (1%)
    pallas_call x4, Pallas kernels, back(): pl.pallas_call(functools.partial(back_kernel, chunk, which_d), out_shape=...  15.7 us
    ppermute x18, starting transfers between devices, swap(): return lax.ppermute(value, axis, [(s, s ^ bit) for s in range(count)])  15.4 us
    pallas_call x2, Pallas kernels, near(): pl.pallas_call(functools.partial(near_kernel, chunk), out_shape=(jax.Shap...  12.3 us
    ppermute x6, starting transfers between devices, later(): lax.ppermute(value, axis, [(s, (s + ROW) % count) for s in range(count)])  10 us
    ppermute x18, waiting for transfers between devices, swap(): return lax.ppermute(value, axis, [(s, s ^ bit) for s in range(count)])  8.1 us
    pallas_call x2, Pallas kernels, far(): pl.pallas_call(functools.partial(far_kernel, chunk, last), out_shape=(jax...  6.68 us
    unnamed x22, local copies, waits for them, and re-layouts  6.64 us
    ppermute x3, starting transfers between devices, shards(): weight_grad += lax.ppermute(terms[delta], 'span', pairs).astype(F32)  6.25 us
  transfers between devices with their start and end apart: 27, of which 7 were waited for; matrix products, arithmetic and copies ran while one was open for 1% of the time, Pallas kernels for 41%

profile of v2, /device:TPU:11, one launch (start us, length us, event | category | flops | bytes accessed | tf_op | source)
XLA Modules:
  0.0 95.9 jit_solution(12953066668971509549)
XLA Ops:
  0.6 0.0 copy-start.2
  0.7 1.1 %copy-done.2 = bf16[256,1024]{1,0:T(8,128)(2,1)S(1)} copy-done((bf16[256,1024]{1,0:T(8,128)(2,1)S(1)}, bf16[256,1024]{1,0:T(8,128)(2,1)}, u32[]{:S(2)}) %copy-start.2) | copy-done | bytes 524312
  1.7 1.0 %copy-done.4 = bf16[256,1024]{1,0:T(8,128)(2,1)S(1)} copy-done((bf16[256,1024]{1,0:T(8,128)(2,1)S(1)}, bf16[256,1024]{1,0:T(8,128)(2,1)}, u32[]{:S(2)}) %copy-start.4) | copy-done | bytes 524312
  2.8 0.4 pack_first.1
  3.2 0.7 collective-permute-start
  3.9 1.3 %collective-permute-start.1 = (bf16[512,128]{1,0:T(8,128)(2,1)S(1)}, bf16[512,128]{1,0:T(8,128)(2,1)S(1)}, u32[]{:S(2)}, u32[]{:S(2)}) collective-permute-start(bf16[512,128]{1,0:T(8,128)(2,1)S(1)} %get-tuple-element.82), channel_id=1, source_target_pairs={{0,2},{1,3},{2,0},{3,1},{4,6},{5,7},{6,4},{7,5},{8,10},{9,11},{10,... | collective-permute-start | bytes 393224 | tf_op jit(solution)/shard_map/ppermute | solution.py:552
  5.2 0.5 collective-permute-start.2
  5.7 1.3 %collective-permute-start.3 = (bf16[1024,128]{1,0:T(8,128)(2,1)S(1)}, bf16[1024,128]{1,0:T(8,128)(2,1)S(1)}, u32[]{:S(2)}, u32[]{:S(2)}) collective-permute-start(bf16[1024,128]{1,0:T(8,128)(2,1)S(1)} %get-tuple-element.87.own0), channel_id=1, source_target_pairs={{0,4},{1,5},{2,6},{3,7},{4,8},{5,9},{6,10},{7,11},{8,12},{9,13},{1... | collective-permute-start | bytes 786440 | tf_op jit(solution)/shard_map/ppermute | solution.py:557
  7.0 0.0 collective-permute-done.a
  7.0 1.0 %copy-done.3 = bf16[256,1024]{1,0:T(8,128)(2,1)S(1)} copy-done((bf16[256,1024]{1,0:T(8,128)(2,1)S(1)}, bf16[256,1024]{1,0:T(8,128)(2,1)}, u32[]{:S(2)}) %copy-start.3) | copy-done | bytes 524312
  8.0 1.0 %copy-done.5 = bf16[256,1024]{1,0:T(8,128)(2,1)S(1)} copy-done((bf16[256,1024]{1,0:T(8,128)(2,1)S(1)}, bf16[256,1024]{1,0:T(8,128)(2,1)}, u32[]{:S(2)}) %copy-start.5) | copy-done | bytes 524312
  9.0 1.0 %copy-done.6 = bf16[256,1024]{1,0:T(8,128)(2,1)S(1)} copy-done((bf16[256,1024]{1,0:T(8,128)(2,1)S(1)}, bf16[256,1024]{1,0:T(8,128)(2,1)}, u32[]{:S(2)}) %copy-start.6) | copy-done | bytes 524312
  10.1 0.7 copy-done.9
  10.8 0.6 pack_second.1
  11.4 0.9 collective-permute-done.2.c
  12.3 1.3 %collective-permute-start.7 = (bf16[1536,128]{1,0:T(8,128)(2,1)S(1)}, bf16[1536,128]{1,0:T(8,128)(2,1)S(1)}, u32[]{:S(2)}, u32[]{:S(2)}) collective-permute-start(bf16[1536,128]{1,0:T(8,128)(2,1)S(1)} %stack.2.rest0), channel_id=1, source_target_pairs={{0,4},{1,5},{2,6},{3,7},{4,8},{5,9},{6,10},{7,11},{8,12},{9,13},{1... | collective-permute-start | bytes 1179656 | tf_op jit(solution)/shard_map/ppermute | solution.py:557
  13.7 0.0 collective-permute-done.3.own1
  13.7 0.7 collective-permute-start.4
  14.4 1.2 %collective-permute-start.5 = (bf16[528,128]{1,0:T(8,128)(2,1)S(1)}, bf16[528,128]{1,0:T(8,128)(2,1)S(1)}, u32[]{:S(2)}, u32[]{:S(2)}) collective-permute-start(bf16[528,128]{1,0:T(8,128)(2,1)S(1)} %get-tuple-element.89), channel_id=1, source_target_pairs={{0,2},{1,3},{2,0},{3,1},{4,6},{5,7},{6,4},{7,5},{8,10},{9,11},{10,... | collective-permute-start | bytes 405512 | tf_op jit(solution)/shard_map/ppermute | solution.py:552
  15.6 0.4 collective-permute-start.6
  16.0 0.0 collective-permute-done.4.a
  16.0 3.6 %collective-permute-done.5.b = bf16[528,128]{1,0:T(8,128)(2,1)S(1)} collective-permute-done((bf16[528,128]{1,0:T(8,128)(2,1)S(1)}, bf16[528,128]{1,0:T(8,128)(2,1)S(1)}, u32[]{:S(2)}, u32[]{:S(2)}) %collective-permute-start.5) | collective-permute-done | bytes 135200 | tf_op jit(solution)/shard_map/ppermute | solution.py:552
  19.6 3.3 %collective-permute-done.6.c = bf16[528,128]{1,0:T(8,128)(2,1)S(1)} collective-permute-done((bf16[528,128]{1,0:T(8,128)(2,1)S(1)}, bf16[528,128]{1,0:T(8,128)(2,1)S(1)}, u32[]{:S(2)}, u32[]{:S(2)}) %collective-permute-start.6) | collective-permute-done | bytes 135200 | tf_op jit(solution)/shard_map/ppermute | solution.py:552
  22.9 0.3 collective-permute-done.7.rest1
  23.2 1.3 %collective-permute-start.8 = (bf16[1536,128]{1,0:T(8,128)(2,1)S(1)}, bf16[1536,128]{1,0:T(8,128)(2,1)S(1)}, u32[]{:S(2)}, u32[]{:S(2)}) collective-permute-start(bf16[1536,128]{1,0:T(8,128)(2,1)S(1)} %stack.3.rest0), channel_id=1, source_target_pairs={{0,4},{1,5},{2,6},{3,7},{4,8},{5,9},{6,10},{7,11},{8,12},{9,13},{1... | collective-permute-start | bytes 1179656 | tf_op jit(solution)/shard_map/ppermute | solution.py:557
  24.6 1.0 %collective-permute-start.10 = (bf16[512,128]{1,0:T(8,128)(2,1)S(1)}, bf16[512,128]{1,0:T(8,128)(2,1)S(1)}, u32[]{:S(2)}, u32[]{:S(2)}) collective-permute-start(bf16[512,128]{1,0:T(8,128)(2,1)S(1)} %get-tuple-element.100), channel_id=1, source_target_pairs={{0,1},{1,0},{2,3},{3,2},{4,5},{5,4},{6,7},{7,6},{8,9},{9,8},{10,11... | collective-permute-start | bytes 393224 | tf_op jit(solution)/shard_map/ppermute | solution.py:552
  25.6 1.2 %collective-permute-start.11 = (bf16[512,128]{1,0:T(8,128)(2,1)S(1)}, bf16[512,128]{1,0:T(8,128)(2,1)S(1)}, u32[]{:S(2)}, u32[]{:S(2)}) collective-permute-start(bf16[512,128]{1,0:T(8,128)(2,1)S(1)} %get-tuple-element.101), channel_id=1, source_target_pairs={{0,2},{1,3},{2,0},{3,1},{4,6},{5,7},{6,4},{7,5},{8,10},{9,11},{10,... | collective-permute-start | bytes 393224 | tf_op jit(solution)/shard_map/ppermute | solution.py:552
  26.8 0.4 collective-permute-start.12
  27.2 0.6 maximum_convert_fusion.track_ref
  27.8 2.3 %plan.1.list_ref.after = s32[8,26]{1,0:T(8,128)} custom-call(s32[8,16]{1,0:T(8,128)} %maximum_convert_fusion.track_ref), custom_call_target="tpu_custom_call" | custom-call | flops 1000000 | bytes 100000 | tf_op jit(solution)/shard_map/plan/pallas_call | solution.py:205
  30.1 3.9 %collective-permute-done.8.rest1 = bf16[1536,128]{1,0:T(8,128)(2,1)S(1)} collective-permute-done((bf16[1536,128]{1,0:T(8,128)(2,1)S(1)}, bf16[1536,128]{1,0:T(8,128)(2,1)S(1)}, u32[]{:S(2)}, u32[]{:S(2)}) %collective-permute-start.8) | collective-permute-done | bytes 393248 | tf_op jit(solution)/shard_map/ppermute | solution.py:557
  34.1 0.0 collective-permute-done.10.s1
  34.1 0.0 collective-permute-done.11.s2
  34.1 1.1 %collective-permute-start.9 = (bf16[1024,128]{1,0:T(8,128)(2,1)S(1)}, bf16[1024,128]{1,0:T(8,128)(2,1)S(1)}, u32[]{:S(2)}, u32[]{:S(2)}) collective-permute-start(bf16[1024,128]{1,0:T(8,128)(2,1)S(1)} %collective-permute-done.3.own1), channel_id=1, source_target_pairs={{0,4},{1,5},{2,6},{3,7},{4,8},{5,9},{6,10},{7,11},{8,12},{9,13},{1... | collective-permute-start | bytes 786440 | tf_op jit(solution)/shard_map/ppermute | solution.py:557
  35.2 1.8 %collective-permute-start.15 = (bf16[1536,128]{1,0:T(8,128)(2,1)S(1)}, bf16[1536,128]{1,0:T(8,128)(2,1)S(1)}, u32[]{:S(2)}, u32[]{:S(2)}) collective-permute-start(bf16[1536,128]{1,0:T(8,128)(2,1)S(1)} %collective-permute-done.7.rest1), channel_id=1, source_target_pairs={{0,4},{1,5},{2,6},{3,7},{4,8},{5,9},{6,10},{7,11},{8,12},{9,13},{1... | collective-permute-start | bytes 1179656 | tf_op jit(solution)/shard_map/ppermute | solution.py:557
  37.0 1.2 %collective-permute-start.13 = (bf16[256,1024]{1,0:T(8,128)(2,1)S(1)}, bf16[256,1024]{1,0:T(8,128)(2,1)S(1)}, u32[]{:S(2)}, u32[]{:S(2)}) collective-permute-start(bf16[256,1024]{1,0:T(8,128)(2,1)S(1)} %copy-done), channel_id=1, source_target_pairs={{0,2},{1,3},{2,0},{3,1},{4,6},{5,7},{6,4},{7,5},{8,10},{9,11},{10,... | collective-permute-start | bytes 1572872 | tf_op jit(solution)/shard_map/ppermute | solution.py:552
  38.2 0.7 copy-done.7
  38.9 6.2 %near0.1 = (f32[3,8,128,128]{3,2,1,0:T(8,128)S(1)}, bf16[29,128,128]{2,1,0:T(8,128)(2,1)S(1)}, bf16[29,128,256]{2,1,0:T(8,128)(2,1)S(1)}, bf16[8,128,128]{2,1,0:T(8,128)(2,1)S(1)}) custom-call(s32[8,26]{1,0:T(8,128)S(1)} %copy-done.7, bf16[1024,128]{1,0:T(8,128)(2,1)S(1)} %get-tuple-element.87.own0, bf16[1536,128]{1,0:T(8,128)(2,1)S(1)} %stack.2.rest0, ...), custom_call_target="tpu_custom_call" | custom-call | flops 6049999872 | bytes 100000 | tf_op jit(solution)/shard_map/near0/pallas_call | solution.py:330
  45.1 6.2 %near1.1 = (f32[3,8,128,128]{3,2,1,0:T(8,128)S(1)}, bf16[29,128,128]{2,1,0:T(8,128)(2,1)S(1)}, bf16[29,128,256]{2,1,0:T(8,128)(2,1)S(1)}, bf16[8,128,128]{2,1,0:T(8,128)(2,1)S(1)}) custom-call(s32[8,26]{1,0:T(8,128)S(1)} %copy-done.7, bf16[1024,128]{1,0:T(8,128)(2,1)S(1)} %get-tuple-element.87.own0, bf16[1536,128]{1,0:T(8,128)(2,1)S(1)} %stack.3.rest0, ...), custom_call_target="tpu_custom_call" | custom-call | flops 1000000 | bytes 100000 | tf_op jit(solution)/shard_map/near1/pallas_call | solution.py:330
  51.3 1.4 %collective-permute-start.16 = (bf16[256,1024]{1,0:T(8,128)(2,1)S(1)}, bf16[256,1024]{1,0:T(8,128)(2,1)S(1)}, u32[]{:S(2)}, u32[]{:S(2)}) collective-permute-start(bf16[256,1024]{1,0:T(8,128)(2,1)S(1)} %copy-done), channel_id=1, source_target_pairs={{0,1},{1,0},{2,3},{3,2},{4,5},{5,4},{6,7},{7,6},{8,9},{9,8},{10,11... | collective-permute-start | bytes 1572872 | tf_op jit(solution)/shard_map/ppermute | solution.py:552
  52.7 0.1 collective-permute-start.17
  52.7 3.0 %far0.1 = (bf16[29,128,128]{2,1,0:T(8,128)(2,1)S(1)}, bf16[29,128,256]{2,1,0:T(8,128)(2,1)S(1)}, bf16[1024,128]{1,0:T(8,128)(2,1)S(1)}, f32[8,128,128]{2,1,0:T(8,128)S(1)}) custom-call(s32[8,26]{1,0:T(8,128)S(1)} %copy-done.7, bf16[1024,128]{1,0:T(8,128)(2,1)S(1)} %collective-permute-done.9.own2, ...), custom_call_target="tpu_custom_call", output_to_operand_aliasing={{0}: (5, {}), {1}: (6, {})} | custom-call | flops 4620000256 | bytes 100000 | tf_op jit(solution)/shard_map/far0/pallas_call | solution.py:408
  55.7 0.0 copy-start.8
  55.7 3.1 %collective-permute-start.14 = (bf16[1536,128]{1,0:T(8,128)(2,1)S(1)}, bf16[1536,128]{1,0:T(8,128)(2,1)S(1)}, u32[]{:S(2)}, u32[]{:S(2)}) collective-permute-start(bf16[1536,128]{1,0:T(8,128)(2,1)S(1)} %collective-permute-done.8.rest1), channel_id=1, source_target_pairs={{0,4},{1,5},{2,6},{3,7},{4,8},{5,9},{6,10},{7,11},{8,12},{9,13},{1... | collective-permute-start | bytes 1179656 | tf_op jit(solution)/shard_map/ppermute | solution.py:557
  58.8 0.8 grad_attn.1.g_ref
  59.6 7.1 %back0_0.1 = (bf16[768,128]{1,0:T(8,128)(2,1)S(1)}, bf16[768,128]{1,0:T(8,128)(2,1)S(1)}, bf16[768,128]{1,0:T(8,128)(2,1)S(1)}, bf16[768,128]{1,0:T(8,128)(2,1)S(1)}) custom-call(s32[8,26]{1,0:T(8,128)S(1)} %copy-done.8, bf16[29,128,128]{2,1,0:T(8,128)(2,1)S(1)} %get-tuple-element.115.kk, bf16[29,128,256]{2,1,0:T(8,128)(2,1)S(1)} %get-tuple-element.116.vv, ...), custom_call_target="tpu_custom_call" | custom-call | flops 9240000512 | bytes 100000 | tf_op jit(solution)/shard_map/back0_0/pallas_call | solution.py:506
  66.7 0.8 collective-permute-start.18
  67.5 0.3 collective-permute-start.19
  67.8 1.4 %collective-permute-start.20 = (bf16[768,128]{1,0:T(8,128)(2,1)S(1)}, bf16[768,128]{1,0:T(8,128)(2,1)S(1)}, u32[]{:S(2)}, u32[]{:S(2)}) collective-permute-start(bf16[768,128]{1,0:T(8,128)(2,1)S(1)} %get-tuple-element.133), channel_id=1, source_target_pairs={{0,3},{1,2},{2,1},{3,0},{4,7},{5,6},{6,5},{7,4},{8,11},{9,10},{10,... | collective-permute-start | bytes 589832 | tf_op jit(solution)/shard_map/ppermute | solution.py:552
  69.2 3.7 %far1.1 = (bf16[29,128,128]{2,1,0:T(8,128)(2,1)S(1)}, bf16[29,128,256]{2,1,0:T(8,128)(2,1)S(1)}, bf16[1024,128]{1,0:T(8,128)(2,1)S(1)}, f32[8,128,128]{2,1,0:T(8...) custom-call(s32[8,26]{1,0:T(8,128)S(1)} %copy-done.8, ...), custom_call_target="tpu_custom_call", output_to_operand_aliasing={{0}: (5, {}), {1}: (6, {})} | custom-call | flops 1000000 | bytes 100000 | tf_op jit(solution)/shard_map/far1/pallas_call | solution.py:408
  73.0 2.3 %collective-permute-start.24 = (bf16[64,1024]{1,0:T(8,128)(2,1)S(1)}, bf16[64,1024]{1,0:T(8,128)(2,1)S(1)}, u32[]{:S(2)}, u32[]{:S(2)}) collective-permute-start(bf16[64,1024]{1,0:T(8,128)(2,1)S(1)} %get-tuple-element.147), channel_id=1, source_target_pairs={{0,4},{1,5},{2,6},{3,7},{4,8},{5,9},{6,10},{7,11},{8,12},{9,13},{1... | collective-permute-start | bytes 393224 | tf_op jit(solution)/shard_map/ppermute | solution.py:617
  75.2 2.6 %collective-permute-start.25 = (bf16[64,1024]{1,0:T(8,128)(2,1)S(1)}, bf16[64,1024]{1,0:T(8,128)(2,1)S(1)}, u32[]{:S(2)}, u32[]{:S(2)}) collective-permute-start(bf16[64,1024]{1,0:T(8,128)(2,1)S(1)} %get-tuple-element.148), channel_id=1, source_target_pairs={{0,8},{1,9},{2,10},{3,11},{4,12},{5,13},{6,14},{7,15},{8,0},{9,1},... | collective-permute-start | bytes 393224 | tf_op jit(solution)/shard_map/ppermute | solution.py:617
  77.8 1.4 %collective-permute-start.26 = (bf16[64,1024]{1,0:T(8,128)(2,1)S(1)}, bf16[64,1024]{1,0:T(8,128)(2,1)S(1)}, u32[]{:S(2)}, u32[]{:S(2)}) collective-permute-start(bf16[64,1024]{1,0:T(8,128)(2,1)S(1)} %get-tuple-element.149), channel_id=1, source_target_pairs={{0,12},{1,13},{2,14},{3,15},{4,0},{5,1},{6,2},{7,3},{8,4},{9,5},{1... | collective-permute-start | bytes 393224 | tf_op jit(solution)/shard_map/ppermute | solution.py:617
  79.2 3.9 %back1_2.1 = (bf16[768,128]{1,0:T(8,128)(2,1)S(1)}, bf16[768,128]{1,0:T(8,128)(2,1)S(1)}) custom-call(s32[8,26]{1,0:T(8,128)S(1)} %copy-done.8, bf16[29,128,128]{2,1,0:T(8,128)(2,1)S(1)} %get-tuple-element.125.kk, bf16[29,128,256]{2,1,0:T(8,128)(2,1)S(1)} %get-tuple-element.126.vv, bf16[8,128,128]{2,1,0:T(8,128)(2,1)S(1)} %get-tuple-element.124.qq, ...), custom_call_target="tpu_custom_call" | custom-call | flops 1000000 | bytes 100000 | tf_op jit(solution)/shard_map/back1_2/pallas_call | solution.py:506
  83.2 1.3 %collective-permute-start.22 = (bf16[768,128]{1,0:T(8,128)(2,1)S(1)}, bf16[768,128]{1,0:T(8,128)(2,1)S(1)}, u32[]{:S(2)}, u32[]{:S(2)}) collective-permute-start(bf16[768,128]{1,0:T(8,128)(2,1)S(1)} %get-tuple-element.135.after), channel_id=1, source_target_pairs={{0,2},{1,3},{2,0},{3,1},{4,6},{5,7},{6,4},{7,5},{8,10},{9,11},{10,... | collective-permute-start | bytes 589832 | tf_op jit(solution)/shard_map/ppermute | solution.py:552
  84.5 2.3 %back1_1.1 = bf16[768,128]{1,0:T(8,128)(2,1)S(1)} custom-call(s32[8,26]{1,0:T(8,128)S(1)} %copy-done.8, bf16[29,128,128]{2,1,0:T(8,128)(2,1)S(1)} %get-tuple-element.125.kk, bf16[29,128,256]{2,1,0:T(8,128)(2,1)S(1)} %get-tuple-element.126.vv, bf16[8,128,128]{2,1,0:T(8,128)(2,1)S(1)} %get-tuple-element.124.qq, bf16[1024,256]{1,0:T(8,128)(2,1)S(1)} %grad_attn.1.g_ref, ...), custom_call_target="tpu_custom_call" | custom-call | flops 1000000 | bytes 100000 | tf_op jit(solution)/shard_map/back1_1/pallas_call | solution.py:506
  86.8 1.3 %collective-permute-start.21 = (bf16[768,128]{1,0:T(8,128)(2,1)S(1)}, bf16[768,128]{1,0:T(8,128)(2,1)S(1)}, u32[]{:S(2)}, u32[]{:S(2)}) collective-permute-start(bf16[768,128]{1,0:T(8,128)(2,1)S(1)} %back1_1.1), channel_id=1, source_target_pairs={{0,1},{1,0},{2,3},{3,2},{4,5},{5,4},{6,7},{7,6},{8,9},{9,8},{10,11... | collective-permute-start | bytes 589832 | tf_op jit(solution)/shard_map/ppermute | solution.py:552
  88.1 0.2 collective-permute-start.23
  88.3 1.8 %collective-permute-done.26 = bf16[64,1024]{1,0:T(8,128)(2,1)S(1)} collective-permute-done((bf16[64,1024]{1,0:T(8,128)(2,1)S(1)}, bf16[64,1024]{1,0:T(8,128)(2,1)S(1)}, u32[]{:S(2)}, u32[]{:S(2)}) %collective-permute-start.26) | collective-permute-done | bytes 131104 | tf_op jit(solution)/shard_map/ppermute | solution.py:617
  90.2 0.8 convert_add_fusion
  90.9 2.3 %back1_0.1.refs_0_ = bf16[768,128]{1,0:T(8,128)(2,1)S(1)} custom-call(s32[8,26]{1,0:T(8,128)S(1)} %copy-done.8, bf16[29,128,128]{2,1,0:T(8,128)(2,1)S(1)} %get-tuple-element.125.kk, bf16[29,128,256]{2,1,0:T(8,128)(2,1)S(1)} %get-tuple-element.126.vv, bf16[8,128,128]{2,1,0:T(8,128)(2,1)S(1)} %get-tuple-element.124.qq, bf16[1024,256]{1,0:T(8,128)(2,1)S(1)} %grad_attn.1.g_ref, ...), custom_call_target="tpu_custom_call" | custom-call | flops 1000000 | bytes 100000 | tf_op jit(solution)/shard_map/back1_0/pallas_call | solution.py:506
  93.3 1.2 %unpack0.1 = (bf16[256,1024]{1,0:T(8,128)(2,1)}, bf16[256,1024]{1,0:T(8,128)(2,1)}, bf16[256,1024]{1,0:T(8,128)(2,1)}) custom-call(bf16[768,128]{1,0:T(8,128)(2,1)S(1)} %get-tuple-element.136.after.refs_0_, bf16[768,128]{1,0:T(8,128)(2,1)S(1)} %collective-permute-done.18.refs_1_, bf16[768,128]{1,0:T(8,128)(2,1)S(1)} %collective-permute-done.19.refs_2_, ...), custom_call_target="tpu_custom_call" | custom-call | flops 1000000 | bytes 100000 | tf_op jit(solution)/shard_map/unpack0/pallas_call | solution.py:537
  94.5 0.3 collective-permute-done.23.refs_3_
  94.7 1.2 %unpack1.1 = (bf16[256,1024]{1,0:T(8,128)(2,1)}, bf16[256,1024]{1,0:T(8,128)(2,1)}, bf16[256,1024]{1,0:T(8,128)(2,1)}) custom-call(bf16[768,128]{1,0:T(8,128)(2,1)S(1)} %back1_0.1.refs_0_, bf16[768,128]{1,0:T(8,128)(2,1)S(1)} %collective-permute-done.21.refs_1_, ...), custom_call_target="tpu_custom_call", output_to_operand_aliasing={{0}: (4, {}), {1}: (5, {}), {2}: (6, {})} | custom-call | flops 1000000 | bytes 100000 | tf_op jit(solution)/shard_map/unpack1/pallas_call | solution.py:537
  (34 shorter events, 0.1 us)
Async XLA Ops:
  0.6 36.4 %copy-start = (bf16[256,1024]{1,0:T(8,128)(2,1)S(1)}, bf16[256,1024]{1,0:T(8,128)(2,1)}, u32[]{:S(2)}) copy-start(bf16[256,1024]{1,0:T(8,128)(2,1)} %refs_1_.1) | copy-start | bytes 1572868
  0.6 1.1 %copy-start.2 = (bf16[256,1024]{1,0:T(8,128)(2,1)S(1)}, bf16[256,1024]{1,0:T(8,128)(2,1)}, u32[]{:S(2)}) copy-start(bf16[256,1024]{1,0:T(8,128)(2,1)} %k_ref.1) | copy-start | bytes 1572868
  1.7 1.0 %copy-start.4 = (bf16[256,1024]{1,0:T(8,128)(2,1)S(1)}, bf16[256,1024]{1,0:T(8,128)(2,1)}, u32[]{:S(2)}) copy-start(bf16[256,1024]{1,0:T(8,128)(2,1)} %v_ref.1) | copy-start | bytes 1572868
  2.8 24.4 %copy-start.10 = (s32[2,16]{1,0:T(2,128)S(1)}, s32[2,16]{1,0:T(2,128)}, u32[]{:S(2)}) copy-start(s32[2,16]{1,0:T(2,128)} %t_ref.1) | copy-start | bytes 388
  3.2 3.8 %collective-permute-start = (bf16[512,128]{1,0:T(8,128)(2,1)S(1)}, bf16[512,128]{1,0:T(8,128)(2,1)S(1)}, u32[]{:S(2)}, u32[]{:S(2)}) collective-permute-start(bf16[512,128]{1,0:T(8,128)(2,1)S(1)} %get-tuple-element.77), channel_id=1, source_target_pairs={{0,1},{1,0},{2,3},{3,2},{4,5},{5,4},{6,7},{7,6},{8,9},{9,8},{10,11... | collective-permute-start | bytes 393224 | tf_op jit(solution)/shard_map/ppermute | solution.py:552
  3.9 7.4 %collective-permute-start.1 = (bf16[512,128]{1,0:T(8,128)(2,1)S(1)}, bf16[512,128]{1,0:T(8,128)(2,1)S(1)}, u32[]{:S(2)}, u32[]{:S(2)}) collective-permute-start(bf16[512,128]{1,0:T(8,128)(2,1)S(1)} %get-tuple-element.82), channel_id=1, source_target_pairs={{0,2},{1,3},{2,0},{3,1},{4,6},{5,7},{6,4},{7,5},{8,10},{9,11},{10,... | collective-permute-start | bytes 393224 | tf_op jit(solution)/shard_map/ppermute | solution.py:552
  5.2 7.1 %collective-permute-start.2 = (bf16[512,128]{1,0:T(8,128)(2,1)S(1)}, bf16[512,128]{1,0:T(8,128)(2,1)S(1)}, u32[]{:S(2)}, u32[]{:S(2)}) collective-permute-start(bf16[512,128]{1,0:T(8,128)(2,1)S(1)} %get-tuple-element.83), channel_id=1, source_target_pairs={{0,3},{1,2},{2,1},{3,0},{4,7},{5,6},{6,5},{7,4},{8,11},{9,10},{10,... | collective-permute-start | bytes 393224 | tf_op jit(solution)/shard_map/ppermute | solution.py:552
  5.7 8.0 %collective-permute-start.3 = (bf16[1024,128]{1,0:T(8,128)(2,1)S(1)}, bf16[1024,128]{1,0:T(8,128)(2,1)S(1)}, u32[]{:S(2)}, u32[]{:S(2)}) collective-permute-start(bf16[1024,128]{1,0:T(8,128)(2,1)S(1)} %get-tuple-element.87.own0), channel_id=1, source_target_pairs={{0,4},{1,5},{2,6},{3,7},{4,8},{5,9},{6,10},{7,11},{8,12},{9,13},{1... | collective-permute-start | bytes 786440 | tf_op jit(solution)/shard_map/ppermute | solution.py:557
  7.0 1.0 %copy-start.3 = (bf16[256,1024]{1,0:T(8,128)(2,1)S(1)}, bf16[256,1024]{1,0:T(8,128)(2,1)}, u32[]{:S(2)}) copy-start(bf16[256,1024]{1,0:T(8,128)(2,1)} %k_ref.1) | copy-start | bytes 1572868
  8.0 1.0 %copy-start.5 = (bf16[256,1024]{1,0:T(8,128)(2,1)S(1)}, bf16[256,1024]{1,0:T(8,128)(2,1)}, u32[]{:S(2)}) copy-start(bf16[256,1024]{1,0:T(8,128)(2,1)} %v_ref.1) | copy-start | bytes 1572868
  9.0 1.0 %copy-start.6 = (bf16[256,1024]{1,0:T(8,128)(2,1)S(1)}, bf16[256,1024]{1,0:T(8,128)(2,1)}, u32[]{:S(2)}) copy-start(bf16[256,1024]{1,0:T(8,128)(2,1)} %q_ref) | copy-start | bytes 1572868
  10.1 0.7 copy-start.9
  12.3 10.9 %collective-permute-start.7 = (bf16[1536,128]{1,0:T(8,128)(2,1)S(1)}, bf16[1536,128]{1,0:T(8,128)(2,1)S(1)}, u32[]{:S(2)}, u32[]{:S(2)}) collective-permute-start(bf16[1536,128]{1,0:T(8,128)(2,1)S(1)} %stack.2.rest0), channel_id=1, source_target_pairs={{0,4},{1,5},{2,6},{3,7},{4,8},{5,9},{6,10},{7,11},{8,12},{9,13},{1... | collective-permute-start | bytes 1179656 | tf_op jit(solution)/shard_map/ppermute | solution.py:557
  13.7 2.3 %collective-permute-start.4 = (bf16[528,128]{1,0:T(8,128)(2,1)S(1)}, bf16[528,128]{1,0:T(8,128)(2,1)S(1)}, u32[]{:S(2)}, u32[]{:S(2)}) collective-permute-start(bf16[528,128]{1,0:T(8,128)(2,1)S(1)} %get-tuple-element.88), channel_id=1, source_target_pairs={{0,1},{1,0},{2,3},{3,2},{4,5},{5,4},{6,7},{7,6},{8,9},{9,8},{10,11... | collective-permute-start | bytes 405512 | tf_op jit(solution)/shard_map/ppermute | solution.py:552
  14.4 5.2 %collective-permute-start.5 = (bf16[528,128]{1,0:T(8,128)(2,1)S(1)}, bf16[528,128]{1,0:T(8,128)(2,1)S(1)}, u32[]{:S(2)}, u32[]{:S(2)}) collective-permute-start(bf16[528,128]{1,0:T(8,128)(2,1)S(1)} %get-tuple-element.89), channel_id=1, source_target_pairs={{0,2},{1,3},{2,0},{3,1},{4,6},{5,7},{6,4},{7,5},{8,10},{9,11},{10,... | collective-permute-start | bytes 405512 | tf_op jit(solution)/shard_map/ppermute | solution.py:552
  15.6 7.3 %collective-permute-start.6 = (bf16[528,128]{1,0:T(8,128)(2,1)S(1)}, bf16[528,128]{1,0:T(8,128)(2,1)S(1)}, u32[]{:S(2)}, u32[]{:S(2)}) collective-permute-start(bf16[528,128]{1,0:T(8,128)(2,1)S(1)} %get-tuple-element.90), channel_id=1, source_target_pairs={{0,3},{1,2},{2,1},{3,0},{4,7},{5,6},{6,5},{7,4},{8,11},{9,10},{10,... | collective-permute-start | bytes 405512 | tf_op jit(solution)/shard_map/ppermute | solution.py:552
  23.2 10.8 %collective-permute-start.8 = (bf16[1536,128]{1,0:T(8,128)(2,1)S(1)}, bf16[1536,128]{1,0:T(8,128)(2,1)S(1)}, u32[]{:S(2)}, u32[]{:S(2)}) collective-permute-start(bf16[1536,128]{1,0:T(8,128)(2,1)S(1)} %stack.3.rest0), channel_id=1, source_target_pairs={{0,4},{1,5},{2,6},{3,7},{4,8},{5,9},{6,10},{7,11},{8,12},{9,13},{1... | collective-permute-start | bytes 1179656 | tf_op jit(solution)/shard_map/ppermute | solution.py:557
  24.6 9.5 %collective-permute-start.10 = (bf16[512,128]{1,0:T(8,128)(2,1)S(1)}, bf16[512,128]{1,0:T(8,128)(2,1)S(1)}, u32[]{:S(2)}, u32[]{:S(2)}) collective-permute-start(bf16[512,128]{1,0:T(8,128)(2,1)S(1)} %get-tuple-element.100), channel_id=1, source_target_pairs={{0,1},{1,0},{2,3},{3,2},{4,5},{5,4},{6,7},{7,6},{8,9},{9,8},{10,11... | collective-permute-start | bytes 393224 | tf_op jit(solution)/shard_map/ppermute | solution.py:552
  25.6 8.5 %collective-permute-start.11 = (bf16[512,128]{1,0:T(8,128)(2,1)S(1)}, bf16[512,128]{1,0:T(8,128)(2,1)S(1)}, u32[]{:S(2)}, u32[]{:S(2)}) collective-permute-start(bf16[512,128]{1,0:T(8,128)(2,1)S(1)} %get-tuple-element.101), channel_id=1, source_target_pairs={{0,2},{1,3},{2,0},{3,1},{4,6},{5,7},{6,4},{7,5},{8,10},{9,11},{10,... | collective-permute-start | bytes 393224 | tf_op jit(solution)/shard_map/ppermute | solution.py:552
  26.8 7.3 %collective-permute-start.12 = (bf16[512,128]{1,0:T(8,128)(2,1)S(1)}, bf16[512,128]{1,0:T(8,128)(2,1)S(1)}, u32[]{:S(2)}, u32[]{:S(2)}) collective-permute-start(bf16[512,128]{1,0:T(8,128)(2,1)S(1)} %get-tuple-element.102), channel_id=1, source_target_pairs={{0,3},{1,2},{2,1},{3,0},{4,7},{5,6},{6,5},{7,4},{8,11},{9,10},{10,... | collective-permute-start | bytes 393224 | tf_op jit(solution)/shard_map/ppermute | solution.py:552
  34.1 18.7 %collective-permute-start.9 = (bf16[1024,128]{1,0:T(8,128)(2,1)S(1)}, bf16[1024,128]{1,0:T(8,128)(2,1)S(1)}, u32[]{:S(2)}, u32[]{:S(2)}) collective-permute-start(bf16[1024,128]{1,0:T(8,128)(2,1)S(1)} %collective-permute-done.3.own1), channel_id=1, source_target_pairs={{0,4},{1,5},{2,6},{3,7},{4,8},{5,9},{6,10},{7,11},{8,12},{9,13},{1... | collective-permute-start | bytes 786440 | tf_op jit(solution)/shard_map/ppermute | solution.py:557
  35.2 17.6 %collective-permute-start.15 = (bf16[1536,128]{1,0:T(8,128)(2,1)S(1)}, bf16[1536,128]{1,0:T(8,128)(2,1)S(1)}, u32[]{:S(2)}, u32[]{:S(2)}) collective-permute-start(bf16[1536,128]{1,0:T(8,128)(2,1)S(1)} %collective-permute-done.7.rest1), channel_id=1, source_target_pairs={{0,4},{1,5},{2,6},{3,7},{4,8},{5,9},{6,10},{7,11},{8,12},{9,13},{1... | collective-permute-start | bytes 1179656 | tf_op jit(solution)/shard_map/ppermute | solution.py:557
  37.0 14.3 %collective-permute-start.13 = (bf16[256,1024]{1,0:T(8,128)(2,1)S(1)}, bf16[256,1024]{1,0:T(8,128)(2,1)S(1)}, u32[]{:S(2)}, u32[]{:S(2)}) collective-permute-start(bf16[256,1024]{1,0:T(8,128)(2,1)S(1)} %copy-done), channel_id=1, source_target_pairs={{0,2},{1,3},{2,0},{3,1},{4,6},{5,7},{6,4},{7,5},{8,10},{9,11},{10,... | collective-permute-start | bytes 1572872 | tf_op jit(solution)/shard_map/ppermute | solution.py:552
  38.2 0.7 copy-start.7
  51.3 7.5 %collective-permute-start.16 = (bf16[256,1024]{1,0:T(8,128)(2,1)S(1)}, bf16[256,1024]{1,0:T(8,128)(2,1)S(1)}, u32[]{:S(2)}, u32[]{:S(2)}) collective-permute-start(bf16[256,1024]{1,0:T(8,128)(2,1)S(1)} %copy-done), channel_id=1, source_target_pairs={{0,1},{1,0},{2,3},{3,2},{4,5},{5,4},{6,7},{7,6},{8,9},{9,8},{10,11... | collective-permute-start | bytes 1572872 | tf_op jit(solution)/shard_map/ppermute | solution.py:552
  52.7 6.2 %collective-permute-start.17 = (bf16[256,1024]{1,0:T(8,128)(2,1)S(1)}, bf16[256,1024]{1,0:T(8,128)(2,1)S(1)}, u32[]{:S(2)}, u32[]{:S(2)}) collective-permute-start(bf16[256,1024]{1,0:T(8,128)(2,1)S(1)} %collective-permute-done.13.g2.refs_3_), channel_id=1, source_target_pairs={{0,1},{1,0},{2,3},{3,2},{4,5},{5,4},{6,7},{7,6},{8,9},{9,8},{10,11... | collective-permute-start | bytes 1572872 | tf_op jit(solution)/shard_map/ppermute | solution.py:552
  52.7 6.1 %copy-start.1 = (bf16[1024,1024]{1,0:T(8,128)(2,1)S(1)}, bf16[1024,1024]{1,0:T(8,128)(2,1)}, u32[]{:S(2)}) copy-start(bf16[1024,1024]{1,0:T(8,128)(2,1)} %w.1) | copy-start | bytes 6291460
  55.7 3.9 %copy-start.8 = (s32[8,26]{1,0:T(8,128)S(1)}, s32[8,26]{1,0:T(8,128)}, u32[]{:S(2)}) copy-start(s32[8,26]{1,0:T(8,128)} %plan.1.list_ref.after) | copy-start | bytes 2500
  55.7 13.5 %collective-permute-start.14 = (bf16[1536,128]{1,0:T(8,128)(2,1)S(1)}, bf16[1536,128]{1,0:T(8,128)(2,1)S(1)}, u32[]{:S(2)}, u32[]{:S(2)}) collective-permute-start(bf16[1536,128]{1,0:T(8,128)(2,1)S(1)} %collective-permute-done.8.rest1), channel_id=1, source_target_pairs={{0,4},{1,5},{2,6},{3,7},{4,8},{5,9},{6,10},{7,11},{8,12},{9,13},{1... | collective-permute-start | bytes 1179656 | tf_op jit(solution)/shard_map/ppermute | solution.py:557
  66.7 11.1 %collective-permute-start.18 = (bf16[768,128]{1,0:T(8,128)(2,1)S(1)}, bf16[768,128]{1,0:T(8,128)(2,1)S(1)}, u32[]{:S(2)}, u32[]{:S(2)}) collective-permute-start(bf16[768,128]{1,0:T(8,128)(2,1)S(1)} %get-tuple-element.131), channel_id=1, source_target_pairs={{0,1},{1,0},{2,3},{3,2},{4,5},{5,4},{6,7},{7,6},{8,9},{9,8},{10,11... | collective-permute-start | bytes 589832 | tf_op jit(solution)/shard_map/ppermute | solution.py:552
  67.5 15.6 %collective-permute-start.19 = (bf16[768,128]{1,0:T(8,128)(2,1)S(1)}, bf16[768,128]{1,0:T(8,128)(2,1)S(1)}, u32[]{:S(2)}, u32[]{:S(2)}) collective-permute-start(bf16[768,128]{1,0:T(8,128)(2,1)S(1)} %get-tuple-element.132), channel_id=1, source_target_pairs={{0,2},{1,3},{2,0},{3,1},{4,6},{5,7},{6,4},{7,5},{8,10},{9,11},{10,... | collective-permute-start | bytes 589832 | tf_op jit(solution)/shard_map/ppermute | solution.py:552
  67.8 15.4 %collective-permute-start.20 = (bf16[768,128]{1,0:T(8,128)(2,1)S(1)}, bf16[768,128]{1,0:T(8,128)(2,1)S(1)}, u32[]{:S(2)}, u32[]{:S(2)}) collective-permute-start(bf16[768,128]{1,0:T(8,128)(2,1)S(1)} %get-tuple-element.133), channel_id=1, source_target_pairs={{0,3},{1,2},{2,1},{3,0},{4,7},{5,6},{6,5},{7,4},{8,11},{9,10},{10,... | collective-permute-start | bytes 589832 | tf_op jit(solution)/shard_map/ppermute | solution.py:552
  73.0 15.2 %collective-permute-start.24 = (bf16[64,1024]{1,0:T(8,128)(2,1)S(1)}, bf16[64,1024]{1,0:T(8,128)(2,1)S(1)}, u32[]{:S(2)}, u32[]{:S(2)}) collective-permute-start(bf16[64,1024]{1,0:T(8,128)(2,1)S(1)} %get-tuple-element.147), channel_id=1, source_target_pairs={{0,4},{1,5},{2,6},{3,7},{4,8},{5,9},{6,10},{7,11},{8,12},{9,13},{1... | collective-permute-start | bytes 393224 | tf_op jit(solution)/shard_map/ppermute | solution.py:617
  75.2 13.1 %collective-permute-start.25 = (bf16[64,1024]{1,0:T(8,128)(2,1)S(1)}, bf16[64,1024]{1,0:T(8,128)(2,1)S(1)}, u32[]{:S(2)}, u32[]{:S(2)}) collective-permute-start(bf16[64,1024]{1,0:T(8,128)(2,1)S(1)} %get-tuple-element.148), channel_id=1, source_target_pairs={{0,8},{1,9},{2,10},{3,11},{4,12},{5,13},{6,14},{7,15},{8,0},{9,1},... | collective-permute-start | bytes 393224 | tf_op jit(solution)/shard_map/ppermute | solution.py:617
  77.8 12.3 %collective-permute-start.26 = (bf16[64,1024]{1,0:T(8,128)(2,1)S(1)}, bf16[64,1024]{1,0:T(8,128)(2,1)S(1)}, u32[]{:S(2)}, u32[]{:S(2)}) collective-permute-start(bf16[64,1024]{1,0:T(8,128)(2,1)S(1)} %get-tuple-element.149), channel_id=1, source_target_pairs={{0,12},{1,13},{2,14},{3,15},{4,0},{5,1},{6,2},{7,3},{8,4},{9,5},{1... | collective-permute-start | bytes 393224 | tf_op jit(solution)/shard_map/ppermute | solution.py:617
  83.2 11.6 %collective-permute-start.22 = (bf16[768,128]{1,0:T(8,128)(2,1)S(1)}, bf16[768,128]{1,0:T(8,128)(2,1)S(1)}, u32[]{:S(2)}, u32[]{:S(2)}) collective-permute-start(bf16[768,128]{1,0:T(8,128)(2,1)S(1)} %get-tuple-element.135.after), channel_id=1, source_target_pairs={{0,2},{1,3},{2,0},{3,1},{4,6},{5,7},{6,4},{7,5},{8,10},{9,11},{10,... | collective-permute-start | bytes 589832 | tf_op jit(solution)/shard_map/ppermute | solution.py:552
  86.8 7.7 %collective-permute-start.21 = (bf16[768,128]{1,0:T(8,128)(2,1)S(1)}, bf16[768,128]{1,0:T(8,128)(2,1)S(1)}, u32[]{:S(2)}, u32[]{:S(2)}) collective-permute-start(bf16[768,128]{1,0:T(8,128)(2,1)S(1)} %back1_1.1), channel_id=1, source_target_pairs={{0,1},{1,0},{2,3},{3,2},{4,5},{5,4},{6,7},{7,6},{8,9},{9,8},{10,11... | collective-permute-start | bytes 589832 | tf_op jit(solution)/shard_map/ppermute | solution.py:552
  88.1 6.6 %collective-permute-start.23 = (bf16[768,128]{1,0:T(8,128)(2,1)S(1)}, bf16[768,128]{1,0:T(8,128)(2,1)S(1)}, u32[]{:S(2)}, u32[]{:S(2)}) collective-permute-start(bf16[768,128]{1,0:T(8,128)(2,1)S(1)} %get-tuple-element.134.after), channel_id=1, source_target_pairs={{0,3},{1,2},{2,1},{3,0},{4,7},{5,6},{6,5},{7,4},{8,11},{9,10},{10,... | collective-permute-start | bytes 589832 | tf_op jit(solution)/shard_map/ppermute | solution.py:552
